TPU v7x, 32 devices: a whole 2x2x4 slice. The times are simulated.
32 devices in a mesh: pb: 2 (over x), ka: 16 (over z, y, core).
Axes of the slice: x: 2, y: 2, z: 4, core: 2. Of those that a mesh axis runs over, the one named last changes fastest.
Arguments:
- tokens: bfloat16 [4096, 768], P(('pb', 'ka')), may hold values from -6 to 6
- positions: float32 [3, 4096], replicated, may hold values from -24 to 24
- item_of_atom: int32 [4096], replicated, may hold values from 0 to 104, as said below
- item_lengths: int32 [105], replicated, may hold values from 8 to 768, as said below
- atom_types: int32 [4096], replicated, may hold values from 0 to 127, as said below
- key_mask: int32 [4096], replicated, may hold values 0 or 1
- ln1_gain: float32 [768], replicated, may hold values from 0.5 to 1.5
- ln1_bias: float32 [768], replicated, may hold values from -3 to 3
- w_qkv: bfloat16 [768, 2304], replicated, may hold values from -0.21875 to 0.21875
- kernel_means: float32 [128], replicated, may hold values from 0 to 16
- kernel_widths: float32 [128], replicated, may hold values from 0.5 to 4
- kernel_weight: bfloat16 [128, 32], replicated, may hold values from -6 to 6
- type_scale: float32 [160], replicated, may hold values from 0.5 to 1.5
- type_shift: float32 [160], replicated, may hold values from -3 to 3
- w_out: bfloat16 [768, 768], replicated, may hold values from -0.875 to 0.875
- ln2_gain: float32 [768], replicated, may hold values from 0.5 to 1.5
- ln2_bias: float32 [768], replicated, may hold values from -3 to 3
- w_up: bfloat16 [768, 3072], replicated, may hold values from -0.21875 to 0.21875
- w_down: bfloat16 [3072, 768], replicated, may hold values from -0.109375 to 0.109375
- out_cotangent: bfloat16 [4096, 768], P(('pb', 'ka')), may hold values from -6 to 6
Outputs:
- block_out: bfloat16 [4096, 768], P(('pb', 'ka'))
- grad_tokens: float32 [4096, 768], P(('pb', 'ka'))
- grad_positions: float32 [3, 4096], P(None, ('pb', 'ka'))
- grad_ln1_gain: float32 [768], replicated
- grad_ln1_bias: float32 [768], replicated
- grad_w_qkv: float32 [768, 2304], P(None, 'ka')
- grad_kernel_means: float32 [128], replicated
- grad_kernel_widths: float32 [128], replicated
- grad_kernel_weight: float32 [128, 32], replicated
- grad_type_scale: float32 [160], replicated
- grad_type_shift: float32 [160], replicated
- grad_w_out: float32 [768, 768], P(None, 'ka')
- grad_ln2_gain: float32 [768], replicated
- grad_ln2_bias: float32 [768], replicated
- grad_w_up: float32 [768, 3072], P(None, 'ka')
- grad_w_down: float32 [3072, 768], P('ka')
Inputs may be any that keep to these rules, and one draw needn't show every extreme that they name: `item_of_atom`: items are contiguous in atom order: item i holds the item_lengths[i] atoms that follow those of items 0 to i - 1; an item is a protein when it has more than 64 atoms, else a molecule. `item_lengths`: the lengths sum to 4096. `atom_types`: ids of protein atoms lie below 32.
All inputs are finite; a program needn't handle non-finite values.
Results may differ from a plain program's by a relative error of at most 0.017.
Values may be sent and summed in bfloat16 or wider, within the bound.
No kernel may reach another device: no remote copies, remote signals or barrier semaphores. Data moves between devices by JAX's collectives and lax.ppermute only.
A program may use at most 128 MiB of HBM per device.

v0:
```python
import functools
import math

import jax
import jax.numpy as jnp
import numpy as np
from jax import lax
from jax.experimental import pallas as pl
from jax.experimental.pallas import tpu as pltpu
from jax.sharding import PartitionSpec as P

MOL_TYPES = 128
PROT_LEN = 768
MOL_MEAN = 32

LN_EPS = 1e-05
GELU_SLOPE = math.sqrt(2.0 / math.pi)
GELU_CUBE = 0.044715
MASKED = -1e30
ROOT_TWO_PI = math.sqrt(2.0 * math.pi)
LOG2E = math.log2(math.e)
KAPPA = math.sqrt(0.5 * LOG2E)

PAD = 32
GROUP = 8
SPAN = PAD * GROUP
PIECES = 3
WEIGHT_PIECES = 2
CHUNK = 32
HEAD_ROWS = 64
BIAS_ROWS = 64
FEW = 8
MESH = ("pb", "ka")

BF = jnp.bfloat16
F32 = jnp.float32


def shifted(block, axis, distance):
    devices = range(lax.axis_size(axis))
    route = [(i - distance, i) for i in devices if i - distance in devices]
    return lax.ppermute(block, axis, route)


def core_flip(block):
    devices = range(lax.axis_size(MESH))
    return lax.ppermute(block, MESH, [(i, i ^ 1) for i in devices])


class Window:
    def __init__(self, block, sibling=None):
        devices = range(lax.axis_size(MESH))
        levels = len(devices) // 4

        def of(level, rest):
            return level % levels * 4 + rest

        one, two, far = [], [], []
        for i in devices:
            level, chip, core = i // 4, (i >> 1) & 1, i & 1
            odd = level & 1
            one.append((i, of(level + (-1 if odd else 1), i % 4)))
            two.append((i, of(level + (1 if odd else -1), i % 4)))
            far.append((i, of(level + (2 if chip else -2), (1 - chip) * 2 + core)))
        self.block, self.sibling = block, sibling
        self.one = lax.ppermute(block, MESH, one)
        self.two = lax.ppermute(block, MESH, two)
        self.far = lax.ppermute(block, MESH, far)

    def middle(self):
        self.other_chip = [flip_bit(x, "ka", 1) for x in (self.block, self.one, self.two)]
        return self.other_chip

    def finish(self):
        beside, one, two = self.other_chip
        mine = [self.far, self.one, one, self.block, beside, self.two, two]
        came = [core_flip(x) for x in mine if x is not self.block]
        own = core_flip(self.block) if self.sibling is None else self.sibling
        return mine + came[:3] + [own] + came[3:]


class Gathered:
    def __init__(self, block):
        self.own, self.own_sibling = block, core_flip(block)
        self.beside = flip_bit(block, "ka", 1)

    def far(self):
        mine = jnp.stack([self.own, self.beside])
        self.groups = [
            flip_mask(mine, "ka", mask) for mask in range(4, lax.axis_size("ka"), 4)
        ]
        return self.groups

    def finish(self):
        self.beside_sibling = core_flip(self.beside)
        self.siblings = [core_flip(x) for x in self.groups]

    def arrays(self):
        return [
            *(x[None] for x in (self.own, self.own_sibling, self.beside, self.beside_sibling)),
            *self.groups,
            *self.siblings,
        ]

    def masks(self):
        far = range(4, lax.axis_size("ka"), 4)
        return [
            (0,), (1,), (2,), (3,),
            *((mask, mask + 2) for mask in far),
            *((mask + 1, mask + 3) for mask in far),
        ]


SLOTS = (
    (0, 5, 6, 3, 4, 1, 2),
    (6, 5, 4, 3, 2, 1, 0),
    (0, 1, 2, 3, 4, 5, 6),
    (2, 1, 4, 3, 6, 5, 0),
)
SPAN_FIRST, SPAN_LAST, SPAN_CORE, SPAN_CHIP, SPAN_SLOT = 0, 1, 2, 3, 4
SPAN_LOW = 16
SPAN_HIGH = 32
SPAN_ROWS = 48
LANES = 128
SIDE = 16


def flip_bit(block, axis, bit):
    devices = range(lax.axis_size(axis))
    return lax.ppermute(block, axis, [(i, i ^ (1 << bit)) for i in devices])


def bits_of(axis):
    return (lax.axis_size(axis) - 1).bit_length()


def flip_mask(block, axis, mask):
    devices = range(lax.axis_size(axis))
    return lax.ppermute(block, axis, [(i, i ^ mask) for i in devices])


class Sum:
    def __init__(self, kept, sent, stages, left=()):
        self.kept, self.sent, self.stages, self.left = kept, list(sent), list(stages), list(left)
        self.total = None

    def came(self):
        axis, bit, count = self.stages[0][:3]
        partners = range(1, 2**count)
        return [flip_mask(x, axis, p << bit) for x, p in zip(self.sent, partners, strict=True)]

    def plan(self):
        stage = self.stages.pop(0)
        if len(stage) == 4:
            return ("join",)
        if self.stages and self.stages[0][0] == "ka" and self.left:
            bit, count = self.stages[0][1] - 1, self.stages[0][2]
            self.left = [b for b in self.left if not bit <= b < bit + count]
            below = sum(1 for b in self.left if b < bit)
            return ("part", bit, count, 2 ** (len(self.left) - below), 2**below)
        return ("whole",)


def over(axis, first=0):
    return [(axis, bit, 1) for bit in range(first, bits_of(axis))]


def slices_sum(kept, sent, order):
    stages = [("ka", bit + 1, count) for bit, count in order] + over("pb")
    left = [b for bit, count in order[1:] for b in range(bit, bit + count)]
    return Sum(kept, [sent], stages, left)


def columns_sum(kept, sent, order):
    stages = [("pb", 0, 1)] + [("ka", bit + 1, count) for bit, count in order]
    left = [b for bit, count in order for b in range(bit, bit + count)]
    return Sum(kept, [sent], stages + over("pb", 1) + [("pb", 0, 1, "join")], left)


def everywhere_sum(values):
    return Sum(values, [values], over("ka") + over("pb"))


def stage_kernel(plans, counts, side_bit, flat_ref, *refs):
    flat = flat_ref[0]
    refs = list(refs)
    kept_refs = [refs.pop(0) for _ in plans]
    came_refs = [[refs.pop(0) for _ in range(count)] for count in counts]
    for plan, kept, came in zip(plans, kept_refs, came_refs):

        def total(*at):
            value = kept[at].astype(F32)
            for ref in came:
                value = value + ref[at].astype(F32)
            return value

        out = refs.pop(0)
        if plan[0] == "whole":
            out[...] = total(Ellipsis).astype(out.dtype)
        elif plan[0] == "join":
            half = kept.shape[-1]
            side = jnp.right_shift(flat, side_bit) & 1
            out[:, pl.ds(pl.multiple_of(side * half, LANES), half)] = kept[...].astype(F32)
            out[:, pl.ds(pl.multiple_of((1 - side) * half, LANES), half)] = came[0][...].astype(F32)
        else:
            _, bit, count, above, below = plan
            mine = jnp.right_shift(flat, bit + 1) & (2**count - 1)
            outs = [out] + [refs.pop(0) for _ in range(2**count - 1)]
            for i in range(above):
                for j in range(below):
                    for other, ref in enumerate(outs):
                        group = jnp.bitwise_xor(mine, other)
                        ref[i * below + j] = total((i * 2**count + group) * below + j).astype(BF)


def advance(sums, flat_array, name, after=()):
    sums = [one for one in sums if one.stages]
    if not sums:
        return
    came = [one.came() for one in sums]
    plans, shapes, sizes = [], [], []
    for one in sums:
        plan = one.plan()
        shape, dtype, size = one.kept.shape, one.kept.dtype, 1
        if plan[0] == "join":
            shape, dtype = (shape[0], 2 * shape[1]), F32
        elif plan[0] == "part":
            shape, size = (plan[3] * plan[4], *shape[1:]), 2 ** plan[2]
        elif not one.stages:
            dtype = F32
        shapes += [shape_of(shape, dtype)] * size
        plans.append(plan)
        sizes.append(size)
    results = once(
        functools.partial(stage_kernel, plans, [len(x) for x in came], bits_of("ka")),
        (flat_array, *(one.kept for one in sums), *(x for group in came for x in group)),
        shapes,
        [],
        1_000_000_000,
        name,
        {0: pltpu.SMEM},
        after=after,
        room=24,
    )
    results = list(results)
    for one, size in zip(sums, sizes):
        one.kept = results.pop(0)
        one.sent = [results.pop(0) for _ in range(size - 1)] or [one.kept]
        if not one.stages:
            one.total = one.kept
        elif one.kept.ndim == 3 and one.kept.shape[0] == 1 and one.stages[0][0] == "pb":
            one.kept = one.kept.reshape(one.kept.shape[1:])
            one.sent = [one.kept]


def layer_norm(values, ln_gain, ln_shift):
    centre = jnp.mean(values, axis=-1, keepdims=True)
    offsets = values - centre
    spread = jnp.mean(offsets * offsets, axis=-1, keepdims=True)
    return offsets * lax.rsqrt(spread + LN_EPS) * ln_gain + ln_shift


def dot_nn(left, right):
    return lax.dot_general(left, right, (((1,), (0,)), ((), ())), preferred_element_type=F32)


def dot_nt(left, right):
    return lax.dot_general(left, right, (((1,), (1,)), ((), ())), preferred_element_type=F32)


def dot_tn(left, right):
    return lax.dot_general(left, right, (((0,), (0,)), ((), ())), preferred_element_type=F32)


def select_table(head_size):
    column = np.arange(SPAN)
    source = (column // PAD) * head_size + column % PAD
    table = [
        (column[:, None] == (source + off)[None, :]) & (column % PAD < head_size)[None, :]
        for off in (0, 64)
    ]
    return np.stack(table).astype(BF)


def group_windows(groups, head_size):
    out = []
    for g in range(groups):
        start = g * GROUP * head_size
        out.append((start // LANES * LANES, (start % LANES) // 64))
    return out


def place_table(heads, head_size):
    column = np.arange(heads * PAD)
    lane = np.arange(LANES)
    return np.stack(
        [
            (lane[:, None] == (column // PAD)[None, :])
            & (column % PAD == head_size + p)[None, :]
            for p in range(PIECES)
        ]
    ).astype(BF)


def tail_tables(heads, head_size):
    lane, tail = np.arange(LANES), np.arange(2 * LANES)
    into = np.stack(
        [
            (lane[:, None] + p * heads == tail[None, :]) & (lane < heads)[:, None]
            for p in range(2 * PIECES)
        ]
    )
    column = np.arange(heads * PAD)
    piece = column % PAD - head_size
    free = (piece >= 0) & (piece < PIECES)
    lane_of = np.where(free, piece * heads + column // PAD, -1)
    out = np.stack(
        [
            (tail[:, None] == lane_of[None, :]) & free[None, :],
            (tail[:, None] - PIECES * heads == lane_of[None, :]) & free[None, :],
        ]
    )
    return into.astype(BF), out.astype(BF)


def ones_row(heads, head_size):
    column = np.arange(heads * PAD) % PAD
    return ((column >= head_size) & (column < head_size + PIECES)).astype(np.float32)[None]


def head_sum_table(heads):
    column = np.arange(heads * PAD)
    return (column[:, None] // PAD == np.arange(LANES)[None, :]).astype(BF)


def pad_columns(values, select_ref, windows):
    parts = [
        dot_nn(values[:, start : start + SPAN], select_ref[kind]).astype(BF)
        for start, kind in windows
    ]
    return jnp.concatenate(parts, axis=1)


def drop_columns(values, select_ref, windows):
    tiles = {}
    for g, (start, kind) in enumerate(windows):
        part = dot_nt(values[:, g * SPAN : (g + 1) * SPAN], select_ref[kind])
        for k in range(SPAN // LANES):
            tile = part[:, k * LANES : (k + 1) * LANES]
            at = start // LANES + k
            tiles[at] = tiles[at] + tile if at in tiles else tile
    return jnp.concatenate([tiles[at] for at in sorted(tiles)], axis=1).astype(BF)


def drop_turned(values, select_ref, windows):
    tiles = {}
    for g, (start, kind) in enumerate(windows):
        part = dot_nt(select_ref[kind], values[:, g * SPAN : (g + 1) * SPAN])
        for k in range(SPAN // LANES):
            tile = part[k * LANES : (k + 1) * LANES]
            at = start // LANES + k
            tiles[at] = tiles[at] + tile if at in tiles else tile
    return jnp.concatenate([tiles[at] for at in sorted(tiles)], axis=0).astype(BF)


def row_of(ref):
    return jnp.concatenate([ref[k : k + 1, :] for k in range(ref.shape[0])], axis=1)


def split(values, count):
    rest, out = values, []
    for _ in range(count):
        piece = rest.astype(BF)
        rest = rest - piece.astype(F32)
        out.append(piece)
    return out


def norm_parts(values):
    centre = jnp.mean(values, axis=-1, keepdims=True)
    offsets = values - centre
    spread = jnp.mean(offsets * offsets, axis=-1, keepdims=True)
    slope = lax.rsqrt(spread + LN_EPS)
    return offsets * slope, slope


def norm_back(grad, normal, slope, gain):
    inner = grad * gain
    mean = jnp.mean(inner, axis=-1, keepdims=True)
    tilt = jnp.mean(inner * normal, axis=-1, keepdims=True)
    by_gain = jnp.sum(grad * normal, axis=0, keepdims=True)
    by_shift = jnp.sum(grad, axis=0, keepdims=True)
    return slope * (inner - mean - normal * tilt), by_gain, by_shift


def stretched_of(own, other):
    delta = [own[:, i : i + 1] - other[i : i + 1, :] for i in range(3)]
    square = delta[0] * delta[0] + delta[1] * delta[1] + delta[2] * delta[2]
    dist = jnp.sqrt(square + 1.0)
    scales = own[:, 3:4] * other[3:4, :]
    stretched = scales * dist + own[:, 4:5] + other[4:5, :]
    return delta, dist, scales, stretched


def mask_of(own, other, key_is_own):
    same = own[:, 5:6] == other[5:6, :]
    itself = own[:, 7:8] == other[7:8, :]
    is_open = (own[:, 6:7] > 0.5) if key_is_own else (other[6:7, :] > 0.5)
    return jnp.where(same & (is_open | itself), 0.0, MASKED)


def line_atoms(lines):
    line = lax.broadcasted_iota(jnp.int32, (lines, lines // GROUP), 0)
    atom = lax.broadcasted_iota(jnp.int32, (lines, lines // GROUP), 1)
    return jnp.where(line // GROUP == atom, 1.0, 0.0).astype(BF)


def line_heads(lines):
    line = lax.broadcasted_iota(jnp.int32, (lines, SPAN), 0)
    column = lax.broadcasted_iota(jnp.int32, (lines, SPAN), 1)
    return jnp.where(column // PAD == line % GROUP, 1.0, 0.0)


def expand_into(out_ref, padded, groups):
    lines = CHUNK * GROUP
    keep = line_heads(lines).astype(BF)
    spread = line_atoms(lines)
    for g in range(groups):
        for i in range(padded.shape[0] // CHUNK):
            part = padded[i * CHUNK : (i + 1) * CHUNK, g * SPAN : (g + 1) * SPAN]
            out_ref[g, i * lines : (i + 1) * lines, :] = dot_nn(spread, part).astype(BF) * keep


def collapse(values):
    lines = values.shape[0]
    kept = values * line_heads(lines)
    high = kept.astype(BF)
    low = (kept - high.astype(F32)).astype(BF)
    line = lax.broadcasted_iota(jnp.int32, (lines // GROUP, lines), 1)
    atom = lax.broadcasted_iota(jnp.int32, (lines // GROUP, lines), 0)
    gather = jnp.where(line // GROUP == atom, 1.0, 0.0).astype(BF)
    return dot_nn(gather, high) + dot_nn(gather, low)


def fetch(span_ref, refs, out_ref):
    slot = span_ref[SPAN_SLOT + span_ref[SPAN_FIRST, 0] + pl.program_id(0), 0]
    count = len(refs) // 2
    rows = refs[0].shape[0]
    for k in range(count):

        @pl.when(slot == k)
        def _():
            out_ref[:rows] = refs[k][...]
            out_ref[rows:] = refs[count + k][...]


def spots_of(span_ref, rows):
    core = span_ref[SPAN_CORE, 0]
    return [pl.ds(pl.multiple_of(at * rows, rows), rows) for at in (core, 1 - core)]


def spread_mask(mask_ref, mask):
    mask_ref[...] = jnp.broadcast_to(mask[:, None, :], mask_ref.shape)


def reaches(span_ref, first, last, low, high):
    return (span_ref[SPAN_LOW + first, 0] <= high) & (span_ref[SPAN_HIGH + last, 0] >= low)


def head_steps(span_ref, rows, step):
    pair = span_ref[SPAN_FIRST, 0] + pl.program_id(0)
    few = HEAD_ROWS // FEW

    def one(i, carry):
        @pl.when(reaches(span_ref, i * few, i * few + few - 1, 2 * pair, 2 * pair + 1))
        def _():
            step(pl.multiple_of(i * HEAD_ROWS, HEAD_ROWS), HEAD_ROWS)

        return carry

    lax.fori_loop(0, rows // HEAD_ROWS, one, 0)


def kernel_steps(span_ref, first, rows, size, step, skipped):
    pair = span_ref[SPAN_FIRST, 0] + pl.program_id(0)
    few = size // FEW

    def one(i, carry):
        at = pl.multiple_of(i * size, size)
        chunk = first // FEW + i * few
        for half in range(2):
            block = 2 * pair + half
            needed = reaches(span_ref, chunk, chunk + few - 1, block, block)

            @pl.when(needed)
            def _():
                step(at, half)

            @pl.when(jnp.logical_not(needed))
            def _():
                skipped(at, half)

        return carry

    lax.fori_loop(0, rows // size, one, 0)


def side_kernel(
    atoms_blocks,
    flat_ref,
    pos_ref,
    item_ref,
    open_ref,
    type_ref,
    length_ref,
    table_ref,
    means_ref,
    widths_ref,
    kw_ref,
    span_ref,
    other_ref,
    own_ref,
    line_ref,
    tab_ref,
    gw_ref,
    kwt_ref,
    par_ref,
):
    flat = flat_ref[0]
    chips = len(SLOTS[0]) // 2
    first_block = flat // 2 * 2 - 2 * chips
    ids = lax.broadcasted_iota(jnp.int32, (LANES, LANES), 0).astype(F32)
    lane = lax.broadcasted_iota(jnp.int32, (1, LANES), 1)
    tables = []
    for k in range(table_ref.shape[0] // 2):
        rows = split(table_ref[2 * k : 2 * k + 1, :], PIECES)
        rows += split(table_ref[2 * k + 1 : 2 * k + 2, :], PIECES)
        rows += [jnp.zeros((2, LANES), BF)]
        tables.append(jnp.concatenate([row.astype(F32) for row in rows], axis=0).astype(BF))
    flags = [
        jnp.broadcast_to(
            jnp.where(length_ref[k : k + 1, :] > 2 * MOL_MEAN, float(MOL_TYPES), 0.0), (8, LANES)
        ).astype(BF)
        for k in range(length_ref.shape[0])
    ]
    for b in range(other_ref.shape[1] // LANES):
        block = first_block + b
        inside = (block >= 0) & (block < atoms_blocks)
        source = jnp.clip(block, 0, atoms_blocks - 1)
        at = pl.ds(pl.multiple_of(source * LANES, LANES), LANES)
        item = jnp.where(inside, item_ref[pl.ds(source, 1), :].astype(F32), -1.0)
        kind = type_ref[pl.ds(source, 1), :].astype(F32)
        for k, flag in enumerate(flags):
            onehot = jnp.where(ids + float(k * LANES) == item, 1.0, 0.0).astype(BF)
            kind = kind + dot_nn(flag, onehot)[0:1, :]
        found = jnp.zeros((8, LANES), F32)
        for k, table in enumerate(tables):
            onehot = jnp.where(ids + float(k * LANES) == kind, 1.0, 0.0).astype(BF)
            found = found + dot_nn(table, onehot)
        rows = [pos_ref[k : k + 1, at] for k in range(3)]
        rows += [found[0:1] + found[1:2] + found[2:3], found[3:4] + found[4:5] + found[5:6]]
        rows += [item, open_ref[pl.ds(source, 1), :].astype(F32)]
        rows += [(block * LANES + lane).astype(F32), kind]
        rows += [jnp.zeros((SIDE - 9, LANES), F32)]
        side = jnp.concatenate(rows, axis=0)
        other_ref[:, b * LANES : (b + 1) * LANES] = side

        @pl.when(block == flat)
        def _():
            line_ref[...] = side

    line = line_ref[...]
    turned = jnp.transpose(
        jnp.concatenate([line, jnp.zeros((LANES - SIDE, LANES), F32)], axis=0)
    )
    own_ref[...] = turned
    chunks = LANES // FEW
    item_column = jnp.broadcast_to(own_ref[:, 5:6], (LANES, LANES))
    par_ref[...] = item_column
    first_item = par_ref[pl.ds(0, chunks, stride=FEW), :]
    last_item = par_ref[pl.ds(FEW - 1, chunks, stride=FEW), :]

    def count(k, carry):
        row = item_ref[pl.ds(k, 1), :].astype(F32)
        below, upto = carry
        return (
            below + jnp.where(row < first_item, 1.0, 0.0),
            upto + jnp.where(row <= last_item, 1.0, 0.0),
        )

    zero = jnp.zeros((chunks, LANES), F32)
    below, upto = lax.fori_loop(0, atoms_blocks, count, (zero, zero))
    below = jnp.sum(below, axis=1, keepdims=True).astype(jnp.int32)
    upto = jnp.sum(upto, axis=1, keepdims=True).astype(jnp.int32)
    low = jnp.right_shift(below - first_block * LANES, 7)
    high = jnp.right_shift(upto - 1 - first_block * LANES, 7)
    span_ref[SPAN_LOW : SPAN_LOW + chunks, :] = jnp.broadcast_to(low, (chunks, LANES))
    span_ref[SPAN_HIGH : SPAN_HIGH + chunks, :] = jnp.broadcast_to(high, (chunks, LANES))
    row = lax.broadcasted_iota(jnp.int32, (SPAN_LOW, LANES), 0)
    kind = (flat // 2) % 4
    head = jnp.where(row == SPAN_FIRST, jnp.right_shift(low[0:1, :], 1), 0)
    head = head + jnp.where(row == SPAN_LAST, jnp.right_shift(high[chunks - 1 :, :], 1), 0)
    head = head + jnp.where(row == SPAN_CORE, flat % 2, 0)
    head = head + jnp.where(row == SPAN_CHIP, flat // 2, 0)
    for k, slots in enumerate(zip(*SLOTS)):
        slot = sum(jnp.where(kind == which, at, 0) for which, at in enumerate(slots))
        head = head + jnp.where(row == SPAN_SLOT + k, slot, 0)
    span_ref[:SPAN_LOW, :] = head

    def column_of(ref):
        return jnp.transpose(jnp.broadcast_to(ref[...], (LANES, LANES)))

    means, widths = column_of(means_ref), column_of(widths_ref)
    peaks = 1.0 / (ROOT_TWO_PI * widths)
    bend = -(KAPPA * KAPPA) / (widths * widths)
    tab_ref[0] = means
    tab_ref[1] = KAPPA / widths
    tab_ref[2] = LOG2E * jnp.log(peaks)
    tab_ref[3] = bend
    turned_weights = kw_ref[...].astype(F32)
    heads = turned_weights.shape[0]
    filler = jnp.zeros((LANES - heads, LANES), F32)
    wide = jnp.transpose(jnp.concatenate([turned_weights, filler], axis=0))
    weights = wide[:, :heads]
    scaled = weights * (peaks / (widths * widths))[:, :heads]
    gw_ref[...] = jnp.concatenate(split(scaled, WEIGHT_PIECES), axis=1)
    kwt_ref[...] = kw_ref[...]
    lanes = lax.broadcasted_iota(jnp.int32, (LANES, LANES), 1)
    par = wide + jnp.where(lanes == heads, peaks, 0.0)
    par_ref[...] = par + jnp.where(lanes == heads + 1, 1.0 / widths, 0.0)


def bias_kernel(span_ref, own_ref, other_ref, tab_ref, kwt_ref, out_ref, str_ref):
    rows, keys = str_ref.shape
    kernels = tab_ref.shape[1]
    heads = kwt_ref.shape[0]
    half_keys = keys // 2
    str_ref[...] = stretched_of(own_ref[...], other_ref[...])[3]

    def step(at, half):
        columns = slice(half * half_keys, (half + 1) * half_keys)
        block = str_ref[pl.ds(at, BIAS_ROWS), columns]
        for r in range(0, BIAS_ROWS, 2):
            parts = []
            for q in range(2):
                line = jnp.broadcast_to(block[r + q : r + q + 1], (kernels, half_keys))
                z = (line - tab_ref[0]) * tab_ref[1]
                parts.append(jnp.exp2(tab_ref[2] - z * z).astype(BF))
            result = dot_nn(kwt_ref[...], jnp.concatenate(parts, axis=1)) * LOG2E
            out_ref[0, at + r, :, columns] = result[:, :half_keys]
            out_ref[0, at + r + 1, :, columns] = result[:, half_keys:]

    def skipped(at, half):
        columns = slice(half * half_keys, (half + 1) * half_keys)
        out_ref[0, pl.ds(at, BIAS_ROWS), :, columns] = jnp.zeros((BIAS_ROWS, heads, half_keys), F32)

    kernel_steps(span_ref, 0, rows, BIAS_ROWS, step, skipped)


def forward_kernel(
    scale2,
    groups,
    span_ref,
    own_ref,
    other_ref,
    *refs,
):
    token_refs, refs = refs[:14], refs[14:]
    gain_ref, shift_ref, w_ref, select_ref, ones_ref, place_ref, bias_ref, *refs = refs
    att_ref, qaug_ref, lse_ref, kvq_ref, *refs = refs
    qexp_ref, mask_ref, max_ref, sum_ref, acc_ref, lane_ref, both_ref = refs
    step = pl.program_id(0)
    width = groups * SPAN
    tok_ref = token_refs[3]
    rows, model_width = tok_ref.shape
    windows = group_windows(groups, model_width // (groups * GROUP))
    gain, shift = row_of(gain_ref), row_of(shift_ref)

    @pl.when(step == 0)
    def _():
        normed = layer_norm(tok_ref[...].astype(F32), gain, shift).astype(BF)
        query = dot_nn(normed, w_ref[:, :model_width]).astype(BF)
        query = pad_columns(query, select_ref, windows)
        qaug_ref[...] = query
        expand_into(qexp_ref, query, groups)
        max_ref[...] = jnp.full(max_ref.shape, 2.0 * MASKED, F32)
        sum_ref[...] = jnp.zeros(sum_ref.shape, F32)
        acc_ref[...] = jnp.zeros(acc_ref.shape, F32)

    fetch(span_ref, token_refs, both_ref)
    normed = layer_norm(both_ref[...].astype(F32), gain, shift).astype(BF)
    spots = spots_of(span_ref, rows)

    for part in range(3):
        source = (part + 1) % 3 * model_width
        value = dot_nn(normed, w_ref[:, source : source + model_width]).astype(BF)
        value = pad_columns(value, select_ref, windows)
        if part < 2:
            value = value + ones_ref[...].astype(BF)
        for k in range(2):
            kvq_ref[0, spots[k], part * width : (part + 1) * width] = (
                value[k * rows : (k + 1) * rows]
            )
    spread_mask(mask_ref, mask_of(own_ref[...], other_ref[...], False))

    def chunk_step(at, count):
        lines = pl.ds(pl.multiple_of(at * GROUP, HEAD_ROWS * GROUP), count * GROUP)
        mask = mask_ref[pl.ds(at, count)]
        for g in range(groups):
            columns = slice(g * SPAN, (g + 1) * SPAN)
            dots = dot_nt(qexp_ref[g, lines, :], kvq_ref[0, :, columns])
            bias = bias_ref[0, pl.ds(at, count), g * GROUP : (g + 1) * GROUP, :] + mask
            scores = dots * scale2 + bias.reshape(dots.shape)
            old = max_ref[g, lines, :]
            top = jnp.maximum(scores[:, :128], scores[:, 128:])
            new = jnp.maximum(old, jnp.max(top, axis=1, keepdims=True))
            alpha = jnp.exp2(old - new)
            low = jnp.exp2(scores[:, :128] - new)
            high = jnp.exp2(scores[:, 128:] - new)
            max_ref[g, lines, :] = new
            sum_ref[g, lines, :] = sum_ref[g, lines, :] * alpha + (low + high)
            probs = jnp.concatenate([low, high], axis=1).astype(BF)
            values = dot_nn(probs, kvq_ref[0, :, width + g * SPAN : width + (g + 1) * SPAN])
            wide = jnp.concatenate([alpha, alpha], axis=1)
            acc_ref[g, lines, :] = acc_ref[g, lines, :] * wide + values

    head_steps(span_ref, rows, chunk_step)

    @pl.when(step == span_ref[SPAN_LAST, 0] - span_ref[SPAN_FIRST, 0])
    def _():
        lane = lax.broadcasted_iota(jnp.int32, (GROUP, 128), 1)
        head = lax.broadcasted_iota(jnp.int32, (GROUP, 128), 0)

        def finish(i, carry):
            at = pl.multiple_of(i * CHUNK, CHUNK)
            lines = pl.ds(pl.multiple_of(i * CHUNK * GROUP, CHUNK * GROUP), CHUNK * GROUP)
            lanes = jnp.zeros((CHUNK, 128), F32)
            for g in range(groups):
                total = jnp.sum(sum_ref[g, lines, :], axis=1, keepdims=True)
                attended = collapse(acc_ref[g, lines, :] / total)
                att_ref[pl.ds(at, CHUNK), g * SPAN : (g + 1) * SPAN] = attended
                lse = max_ref[g, lines, :] + jnp.log(total) * LOG2E
                own_lane = jnp.where(lane == head + g * GROUP, 1.0, 0.0)
                lanes = lanes + jnp.sum(
                    lse.reshape(CHUNK, GROUP, 128) * own_lane[None], axis=1
                )
            lane_ref[pl.ds(at, CHUNK), :] = lanes
            return carry

        lax.fori_loop(0, rows // CHUNK, finish, 0)
        rest = lane_ref[...] * (-1.0 / scale2)
        query = qaug_ref[...].astype(F32)
        for p in range(PIECES):
            piece = rest.astype(BF)
            rest = rest - piece.astype(F32)
            lse_ref[p] = piece
            query = query + dot_nn(piece, place_ref[p])
        qaug_ref[...] = query.astype(BF)


def query_grad_kernel(
    scale2,
    head_scale,
    groups,
    span_ref,
    own_ref,
    other_ref,
    qaug_ref,
    doaug_ref,
    kv_ref,
    bias_ref,
    select_ref,
    dq_ref,
    ds_ref,
    qexp_ref,
    doexp_ref,
    mask_ref,
    dqacc_ref,
    low_ref,
):
    step = pl.program_id(0)
    width = groups * SPAN
    rows, keys = own_ref.shape[0], other_ref.shape[1]
    windows = group_windows(groups, dq_ref.shape[0] // (groups * GROUP))

    @pl.when(step == 0)
    def _():
        expand_into(qexp_ref, qaug_ref[...], groups)
        expand_into(doexp_ref, doaug_ref[...], groups)
        dqacc_ref[...] = jnp.zeros(dqacc_ref.shape, F32)

    spread_mask(mask_ref, mask_of(own_ref[...], other_ref[...], False))

    def chunk_step(at, count):
        lines = pl.ds(pl.multiple_of(at * GROUP, HEAD_ROWS * GROUP), count * GROUP)
        mask = mask_ref[pl.ds(at, count)]
        waiting = []
        for g in range(groups):
            key_block = kv_ref[0, :, g * SPAN : (g + 1) * SPAN]
            value_block = kv_ref[0, :, width + g * SPAN : width + (g + 1) * SPAN]
            dots = dot_nt(qexp_ref[g, lines, :], key_block)
            grads = dot_nt(doexp_ref[g, lines, :], value_block)
            bias = bias_ref[0, pl.ds(at, count), g * GROUP : (g + 1) * GROUP, :] + mask
            probs = jnp.exp2(dots * scale2 + bias.reshape(dots.shape))
            grad_scores = probs * grads
            dqacc_ref[g, lines, :] += dot_nn(grad_scores.astype(BF), key_block)
            waiting.append(grad_scores.reshape(count, GROUP, keys))
            if len(waiting) == 2:
                ds_ref[0, pl.ds(at, count), (g - 1) * GROUP : (g + 1) * GROUP, :] = (
                    jnp.concatenate(waiting, axis=1).astype(BF)
                )
                waiting = []

    head_steps(span_ref, rows, chunk_step)

    @pl.when(step == span_ref[SPAN_LAST, 0] - span_ref[SPAN_FIRST, 0])
    def _():
        def finish(i, carry):
            at = pl.multiple_of(i * CHUNK, CHUNK)
            lines = pl.ds(pl.multiple_of(i * CHUNK * GROUP, CHUNK * GROUP), CHUNK * GROUP)
            for g in range(groups):
                value = collapse(dqacc_ref[g, lines, :]) * head_scale
                low_ref[pl.ds(at, CHUNK), g * SPAN : (g + 1) * SPAN] = value.astype(BF)
            return carry

        lax.fori_loop(0, rows // CHUNK, finish, 0)
        dq_ref[...] = drop_turned(low_ref[...], select_ref, windows)


def phi_grad_kernel(
    first_row,
    span_ref,
    own_ref,
    other_ref,
    line_ref,
    ds_ref,
    tab_ref,
    kw_ref,
    par_ref,
    small_ref,
    pos_ref,
    str_ref,
    gs_ref,
    own_acc_ref,
    gkw_ref,
    moment_ref,
    type_ref,
):
    step = pl.program_id(0)
    rows, keys = str_ref.shape
    kernels = tab_ref.shape[1]
    heads = gkw_ref.shape[1]
    blocks = pos_ref.shape[0] // 3
    pair_block = 2 * (span_ref[SPAN_CHIP, 0] + span_ref[SPAN_FIRST, 0] + step)

    @pl.when(step == 0)
    def _():
        gkw_ref[...] = jnp.zeros(gkw_ref.shape, F32)
        moment_ref[...] = jnp.zeros(moment_ref.shape, F32)
        own_acc_ref[...] = jnp.zeros(own_acc_ref.shape, F32)
        pos_ref[...] = jnp.zeros(pos_ref.shape, F32)
        type_ref[...] = jnp.zeros(type_ref.shape, F32)

    def add_types(kind, by_scale, by_shift):
        count = type_ref.shape[1]
        onehot = lax.broadcasted_iota(jnp.int32, (count, LANES), 0).astype(F32) == kind
        type_ref[0] += jnp.where(onehot, by_scale, 0.0)
        type_ref[1] += jnp.where(onehot, by_shift, 0.0)

    own, other = own_ref[first_row : first_row + rows, :], other_ref[...]
    str_ref[...] = stretched_of(own, other)[3]

    half_keys = keys // 2

    def pair_step(at, half):
        columns = slice(half * half_keys, (half + 1) * half_keys)
        block = str_ref[pl.ds(at, CHUNK), columns]
        first = second = weights = None
        lines = []
        for r in range(0, CHUNK, 2):
            low = jnp.concatenate([ds_ref[0, at + r + q, :, columns] for q in range(2)], axis=1)
            dphi = dot_nn(kw_ref[...], jnp.concatenate([low] * WEIGHT_PIECES, axis=0))
            phis = []
            for q in range(2):
                away = jnp.broadcast_to(block[r + q : r + q + 1], (kernels, half_keys)) - tab_ref[0]
                phi = jnp.exp2(away * away * tab_ref[3])
                phis.append(phi.astype(BF))
                moved = dphi[:, q * half_keys : (q + 1) * half_keys] * phi * away
                bent = moved * away
                first = moved if first is None else first + moved
                second = bent if second is None else second + bent
                lines.append(jnp.sum(moved, axis=0, keepdims=True))
            part = dot_nt(jnp.concatenate(phis, axis=1), low)
            weights = part if weights is None else weights + part
        moment_ref[0] += first
        moment_ref[1] += second
        gs_ref[pl.ds(at, CHUNK), columns] = jnp.concatenate(lines, axis=0)
        gkw_ref[...] += weights

    def skipped(at, half):
        columns = slice(half * half_keys, (half + 1) * half_keys)
        gs_ref[pl.ds(at, CHUNK), columns] = jnp.zeros((CHUNK, half_keys), F32)

    kernel_steps(span_ref, first_row, rows, CHUNK, pair_step, skipped)

    delta, dist, scales, _ = stretched_of(own, other)
    grad = -gs_ref[...]
    by_scale = grad * dist
    pull = grad * scales / dist
    terms = [pull * delta[0], pull * delta[1], pull * delta[2], by_scale * other[3:4, :], grad]
    for k, term in enumerate(terms):
        own_acc_ref[k] += term[:, :128] + term[:, 128:]
    for half in range(2):
        part = slice(half * LANES, (half + 1) * LANES)
        for k in range(3):
            spot = pl.ds(k * blocks + pair_block + half, 1)
            pos_ref[spot, :] += -jnp.sum(terms[k][:, part], axis=0, keepdims=True)
        add_types(
            other[8:9, part],
            jnp.sum(by_scale[:, part] * own[:, 3:4], axis=0, keepdims=True),
            jnp.sum(grad[:, part], axis=0, keepdims=True),
        )

    @pl.when(step == span_ref[SPAN_LAST, 0] - span_ref[SPAN_FIRST, 0])
    def _():
        lane = lax.broadcasted_iota(jnp.int32, (rows, LANES), 1)
        total = jnp.zeros((rows, LANES), F32)
        for k in range(5):
            column = jnp.sum(own_acc_ref[k], axis=1, keepdims=True)
            total = total + jnp.where(lane == k, column, 0.0)
        rest = [jnp.zeros((count, LANES), F32) for count in (first_row, LANES - first_row - rows)]
        total = jnp.concatenate([x for x in (rest[0], total, rest[1]) if x.shape[0]], axis=0)
        turned = jnp.transpose(total)
        own_block = 2 * (span_ref[SPAN_CHIP, 0] + len(SLOTS[0]) // 2) + span_ref[SPAN_CORE, 0]
        for k in range(3):
            pos_ref[pl.ds(k * blocks + own_block, 1), :] += turned[k : k + 1, :]
        add_types(line_ref[8:9, :], turned[3:4, :], turned[4:5, :])

        par = par_ref[...]
        by_weight = gkw_ref[...] * par[:, heads : heads + 1]
        plain = jnp.sum(by_weight * par[:, :heads], axis=1, keepdims=True)
        by_mean = jnp.sum(moment_ref[0], axis=1, keepdims=True)
        by_width = jnp.sum(moment_ref[1], axis=1, keepdims=True) - plain
        columns = [by_mean, by_width * par[:, heads + 1 : heads + 2]]
        low, high = slice(0, LANES), slice(LANES, 2 * LANES)
        for part in (low, high):
            for k in range(2):
                columns.append(jnp.sum(type_ref[k, part, :], axis=1, keepdims=True))
        lane = lax.broadcasted_iota(jnp.int32, (LANES, LANES), 1)
        wide = jnp.concatenate([by_weight, jnp.zeros((LANES, LANES - heads), F32)], axis=1)
        for k, column in enumerate(columns):
            wide = wide + jnp.where(lane == heads + k, column, 0.0)
        small_ref[...] = wide


def middle_kernel(
    groups,
    tile,
    flat_ref,
    tok_ref,
    att_ref,
    lse_ref,
    gain_ref,
    shift_ref,
    cot_ref,
    wout_hbm,
    wup_hbm,
    wdown_hbm,
    select_ref,
    place_ref,
    sum_ref,
    into_ref,
    out_ref,
    gmix_ref,
    doaug_ref,
    payload_ref,
    attlow_ref,
    normed_ref,
    mine_ref,
    theirs_ref,
    lngrad_ref,
    wout_ref,
    wup_ref,
    wdown_ref,
    down_ref,
    back_ref,
    wout_sem,
    tile_sems,
):
    rows, model_width = tok_ref.shape
    width = groups * SPAN
    windows = group_windows(groups, model_width // (groups * GROUP))
    tiles = wup_ref.shape[1] // tile
    piece = mine_ref.shape[2]
    core = flat_ref[0] % 2

    def tile_copies(t):
        spot = pl.ds(pl.multiple_of(t * tile, LANES), tile)
        return (
            pltpu.make_async_copy(wup_hbm.at[:, spot], wup_ref.at[:, spot], tile_sems.at[0, t]),
            pltpu.make_async_copy(wdown_hbm.at[spot, :], wdown_ref.at[spot, :], tile_sems.at[1, t]),
        )

    first = pltpu.make_async_copy(wout_hbm, wout_ref, wout_sem)
    first.start()
    for t in range(tiles):
        for copy in tile_copies(t):
            copy.start()

    gain, shift = row_of(gain_ref), row_of(shift_ref)
    cotangent = cot_ref[...]
    attended = att_ref[...]
    attended_low = drop_columns(attended.astype(BF), select_ref, windows)
    attlow_ref[...] = attended_low
    first.wait()
    mixed = tok_ref[...].astype(F32) + dot_nn(attended_low, wout_ref[...])
    normal, slope = norm_parts(mixed)
    normed_ref[...] = (normal * gain + shift).astype(BF)
    down_ref[...] = mixed
    back_ref[...] = jnp.zeros(back_ref.shape, F32)

    def step(t, carry):
        for copy in tile_copies(t):
            copy.wait()
        spot = pl.ds(pl.multiple_of(t * tile, LANES), tile)
        up = dot_nn(normed_ref[...], wup_ref[:, spot])
        grad_hidden = dot_nt(cotangent, wdown_ref[spot, :])
        square = up * up
        bent = jnp.tanh(GELU_SLOPE * (up * (1.0 + GELU_CUBE * square)))
        gate = 0.5 * (1.0 + bent)
        inner = GELU_SLOPE * (1.0 + 3.0 * GELU_CUBE * square)
        hidden = (up * gate).astype(BF)
        grad_up = (grad_hidden * (gate + 0.5 * up * (1.0 - bent * bent) * inner)).astype(BF)
        for kind, value in enumerate((grad_up, hidden)):
            value = jnp.transpose(value.astype(F32)).astype(BF)
            for q in range(tile // piece):
                part = value[q * piece : (q + 1) * piece]
                at = t * (tile // piece // 2) + q // 2

                @pl.when(core == q % 2)
                def _():
                    mine_ref[kind, at] = part

                @pl.when(core != q % 2)
                def _():
                    theirs_ref[kind, at] = part

        down_ref[...] += dot_nn(hidden, wdown_ref[spot, :])
        back_ref[...] += dot_nt(grad_up, wup_ref[:, spot])
        return carry

    lax.fori_loop(0, tiles, step, 0)
    out_ref[...] = down_ref[...].astype(BF)
    back, by_gain, by_shift = norm_back(back_ref[...], normal, slope, gain)
    lngrad_ref[...] = jnp.concatenate([by_gain, by_shift], axis=0)
    grad_mixed = cotangent.astype(F32) + back
    gmix_ref[...] = grad_mixed
    grad_low = grad_mixed.astype(BF)
    grad_attended = dot_nt(grad_low, wout_ref[...]).astype(BF)
    padded = pad_columns(grad_attended, select_ref, windows).astype(F32)
    high, low = split(padded * attended, 2)
    delta = dot_nn(high, sum_ref[...]) + dot_nn(low, sum_ref[...])
    pieces = split(-delta, PIECES)
    tail = jnp.zeros((rows, 2 * LANES), F32)
    for p in range(PIECES):
        padded = padded + dot_nn(pieces[p], place_ref[p])
        tail = tail + dot_nn(lse_ref[p], into_ref[p]) + dot_nn(pieces[p], into_ref[PIECES + p])
    doaug_ref[...] = padded.astype(BF)
    payload_ref[:, :model_width] = grad_low
    payload_ref[:, model_width:] = tail.astype(BF)


def weight_grads_kernel(
    ka_count,
    flat_ref,
    mine_ref,
    came_ref,
    normed_ref,
    normed_came_ref,
    cot_ref,
    cot_came_ref,
    attlow_ref,
    attlow_came_ref,
    payload_ref,
    payload_came_ref,
    up_kept_ref,
    up_sent_ref,
    rest_kept_ref,
    rest_sent_ref,
    product_ref,
):
    flat = flat_ref[0]
    core, bit, side = flat % 2, (flat // 2) % 2, (flat // ka_count) % 2
    model_width = normed_ref.shape[1]
    rows = up_kept_ref.shape[1]
    half = model_width // 2
    slices = up_kept_ref.shape[0] * 2
    out_rows = model_width // ka_count
    normed = jnp.concatenate([normed_ref[...], normed_came_ref[...]], axis=0)
    cotangent = jnp.concatenate([cot_ref[...], cot_came_ref[...]], axis=0)

    def columns(which):
        return pl.ds(pl.multiple_of(which * half, LANES), half)

    def step(m, carry):
        both = jnp.concatenate([mine_ref[0, m], came_ref[0, m]], axis=1)
        value = dot_nn(both, normed).astype(BF)

        @pl.when(m % 2 == bit)
        def _():
            up_kept_ref[m // 2] = value

        @pl.when(m % 2 != bit)
        def _():
            up_sent_ref[m // 2] = value

        both = jnp.concatenate([mine_ref[1, m], came_ref[1, m]], axis=1)
        product_ref[:rows, :] = dot_nn(both, cotangent)
        rest_kept_ref[m, :rows, :] = product_ref[:rows, columns(side)].astype(BF)
        rest_sent_ref[m, :rows, :] = product_ref[:rows, columns(1 - side)].astype(BF)
        return carry

    lax.fori_loop(0, slices, step, 0)
    grads = jnp.concatenate(
        [payload_ref[:, :model_width], payload_came_ref[:, :model_width]], axis=0
    )
    attended = jnp.concatenate([attlow_ref[...], attlow_came_ref[...]], axis=0)
    product_ref[...] = dot_tn(grads, attended)

    def out_step(m, carry):
        spot = pl.ds(pl.multiple_of((2 * m + core) * out_rows, 8), out_rows)
        rest_kept_ref[m, rows:, :] = product_ref[spot, columns(side)].astype(BF)
        rest_sent_ref[m, rows:, :] = product_ref[spot, columns(1 - side)].astype(BF)
        return carry

    lax.fori_loop(0, slices, out_step, 0)


def normal_kernel(tok_ref, gain_ref, shift_ref, out_ref):
    normal, _ = norm_parts(tok_ref[...].astype(F32))
    out_ref[...] = (normal * row_of(gain_ref) + row_of(shift_ref)).astype(BF)


def qkv_grads_kernel(masks, groups, *refs):
    grads_refs, normed_refs, out_ref, norm_ref = refs[:groups], refs[groups:-2], refs[-2], refs[-1]
    columns = out_ref.shape[0]
    lefts, rights, parts = [], [], None
    for ref, group in zip(normed_refs, masks):
        for i, mask in enumerate(group):
            grads = grads_refs[mask // 4][mask % 4]
            lefts.append(grads[:columns])
            rights.append(ref[i])
            part = grads[columns:].astype(F32)
            parts = part if parts is None else parts + part
    total = None
    for i in range(0, len(lefts), 2):
        part = dot_nn(
            jnp.concatenate(lefts[i : i + 2], axis=1), jnp.concatenate(rights[i : i + 2], axis=0)
        )
        total = part if total is None else total + part
    out_ref[...] = total.astype(BF)
    norm_ref[...] = parts


def results_kernel(
    heads,
    types,
    flat_ref,
    joined_ref,
    first_ref,
    norm_ref,
    weight_ref,
    mean_ref,
    width_ref,
    scale_ref,
    shift_ref,
    pos_ref,
):
    small = joined_ref[:LANES, :]
    weight_ref[...] = small[:, :heads]
    turned = jnp.transpose(small)
    rows = [turned[heads + k : heads + k + 1, :] for k in range(6)]
    mean_ref[...] = rows[0]
    width_ref[...] = rows[1]
    scale_ref[...] = jnp.concatenate([rows[2], rows[4]], axis=1)[:, :types]
    shift_ref[...] = jnp.concatenate([rows[3], rows[5]], axis=1)[:, :types]
    count = norm_ref.shape[1]
    for k in range(2):
        norm_ref[k] = first_ref[k * count : (k + 1) * count, :]
        norm_ref[2 + k] = joined_ref[LANES + k * count : LANES + (k + 1) * count, :]
    first = LANES + 2 * count
    blocks = (joined_ref.shape[0] - first) // 3
    for k in range(3):
        spot = first + k * blocks + len(SLOTS[0]) // 2 * 2 + flat_ref[0]
        pos_ref[k : k + 1, :] = joined_ref[pl.ds(spot, 1), :]


def first_norm_kernel(
    ka_count,
    flat_ref,
    tok_ref,
    gain_ref,
    dq_ref,
    dkv_ref,
    w_ref,
    gmix_ref,
    grad_ref,
    *refs,
):
    *part_refs, joined_ref = refs
    model_width = tok_ref.shape[1]
    grad = dot_nn(w_ref[:, :model_width], dq_ref[...])
    grad = grad + dot_nn(w_ref[:, model_width:], dkv_ref[...])
    grad = jnp.transpose(grad)
    normal, slope = norm_parts(tok_ref[...].astype(F32))
    back, by_gain, by_shift = norm_back(grad, normal, slope, row_of(gain_ref))
    grad_ref[...] = gmix_ref[...] + back
    lines = [
        row[:, k : k + LANES] for row in (by_gain, by_shift) for k in range(0, model_width, LANES)
    ]
    joined_ref[:model_width, :] = dq_ref[...]
    joined_ref[model_width:, :] = dkv_ref[...]
    here = flat_ref[0] % ka_count
    rows = part_refs[0].shape[1]
    columns = 3 * model_width // ka_count
    lines.append(jnp.zeros((rows - columns - len(lines), LANES), F32))
    lines = jnp.concatenate(lines, axis=0).astype(BF)
    for ref in part_refs:
        for i in range(ka_count // 4):
            ref[i, columns:, :] = lines
    for d in range(ka_count):
        value = joined_ref[d * columns : (d + 1) * columns, :]
        differs = jnp.bitwise_xor(here, d)
        for k, ref in enumerate(part_refs):

            @pl.when(differs % 4 == k)
            def _():
                ref[differs // 4, :columns, :] = value


def regroup_kernel(*refs):
    ins, outs = refs[:4], refs[4:]
    for i, out in enumerate(outs):
        for k, ref in enumerate(ins):
            out[k] = ref[i]


def key_grad_kernel(
    scale2,
    head_scale,
    groups,
    model_width,
    span_ref,
    own_ref,
    other_ref,
    kv_ref,
    q_ref,
    *refs,
):
    payload_refs, refs = refs[:14], refs[14:]
    wout_ref, select_ref, place_ref, bias_ref, dkv_ref, kexp_ref, vexp_ref, *refs = refs
    mask_ref, qb_ref, dob_ref, dk_ref, dv_ref, both_ref, low_ref = refs
    step = pl.program_id(0)
    width = groups * SPAN
    rows = own_ref.shape[0]
    windows = group_windows(groups, model_width // (groups * GROUP))

    @pl.when(step == 0)
    def _():
        expand_into(kexp_ref, kv_ref[0, :, :width], groups)
        expand_into(vexp_ref, kv_ref[0, :, width:], groups)
        dk_ref[...] = jnp.zeros(dk_ref.shape, F32)
        dv_ref[...] = jnp.zeros(dv_ref.shape, F32)

    fetch(span_ref, payload_refs, both_ref)
    payload = both_ref[...]
    tail = payload[:, model_width:]
    grads = dot_nt(payload[:, :model_width], wout_ref[...]).astype(BF)
    grads = pad_columns(grads, select_ref, windows).astype(F32)
    grads = (grads + dot_nn(tail, place_ref[1])).astype(BF)
    shifts = dot_nn(tail, place_ref[0])
    for k, spot in enumerate(spots_of(span_ref, rows)):
        own_part = slice(k * rows, (k + 1) * rows)
        dob_ref[spot, :] = grads[own_part]
        qb_ref[spot, :] = (q_ref[0, spot, :].astype(F32) + shifts[own_part]).astype(BF)
    spread_mask(mask_ref, mask_of(own_ref[...], other_ref[...], True))

    def chunk_step(at, count):
        lines = pl.ds(pl.multiple_of(at * GROUP, HEAD_ROWS * GROUP), count * GROUP)
        mask = mask_ref[pl.ds(at, count)]
        for g in range(groups):
            query_block = qb_ref[:, g * SPAN : (g + 1) * SPAN]
            grad_block = dob_ref[:, g * SPAN : (g + 1) * SPAN]
            dots = dot_nt(kexp_ref[g, lines, :], query_block)
            grads = dot_nt(vexp_ref[g, lines, :], grad_block)
            bias = bias_ref[0, pl.ds(at, count), g * GROUP : (g + 1) * GROUP, :] + mask
            probs = jnp.exp2(dots * scale2 + bias.reshape(dots.shape))
            grad_scores = (probs * grads).astype(BF)
            dk_ref[g, lines, :] += dot_nn(grad_scores, query_block)
            dv_ref[g, lines, :] += dot_nn(probs.astype(BF), grad_block)

    head_steps(span_ref, rows, chunk_step)

    @pl.when(step == span_ref[SPAN_LAST, 0] - span_ref[SPAN_FIRST, 0])
    def _():
        def finish(i, carry):
            at = pl.multiple_of(i * CHUNK, CHUNK)
            lines = pl.ds(pl.multiple_of(i * CHUNK * GROUP, CHUNK * GROUP), CHUNK * GROUP)
            for part, (ref, scale) in enumerate(((dk_ref, head_scale), (dv_ref, 1.0))):
                for g in range(groups):
                    value = collapse(ref[g, lines, :]) * scale
                    low_ref[part, pl.ds(at, CHUNK), g * SPAN : (g + 1) * SPAN] = value.astype(BF)
            return carry

        lax.fori_loop(0, rows // CHUNK, finish, 0)
        for part in range(2):
            dkv_ref[part * model_width : (part + 1) * model_width, :] = drop_turned(
                low_ref[part], select_ref, windows
            )


def fixed(shape):
    return pl.BlockSpec(shape, lambda j, span: (0,) * len(shape), pipeline_mode=pl.Buffered(1))


def pair_at(j, span):
    return jnp.minimum(span[SPAN_FIRST, 0] + j, span[SPAN_LAST, 0])


def moving(shape, rank_at=0, last=0):
    def index(j, span):
        at = [0] * len(shape)
        at[rank_at] = pair_at(j, span)
        if last:
            at[-1] = last
        return tuple(at)

    return pl.BlockSpec(shape, index)


def call(
    kernel, steps, in_specs, out_specs, out_shapes, scratch, flops, name, after=(), carry=(), room=56
):
    extra, given = len(after) + len(carry), len(in_specs)
    single = not isinstance(out_shapes, list)
    if single:
        out_specs, out_shapes = [out_specs], [out_shapes]
    made = len(out_shapes)
    anywhere = pl.BlockSpec(memory_space=pl.ANY)

    def body(span_ref, *refs):
        @pl.when(pl.program_id(0) <= span_ref[SPAN_LAST, 0] - span_ref[SPAN_FIRST, 0])
        def _():
            outs = refs[extra + given : extra + given + made]
            kernel(
                span_ref, *refs[extra : extra + given], *outs, *refs[extra + given + made + len(carry) :]
            )

    inner = pl.pallas_call(
        body,
        grid_spec=pltpu.PrefetchScalarGridSpec(
            num_scalar_prefetch=1,
            grid=(steps,),
            in_specs=[anywhere] * extra + in_specs,
            out_specs=out_specs + [anywhere] * len(carry),
            scratch_shapes=scratch,
        ),
        out_shape=out_shapes + [shape_of(x.shape, x.dtype) for x in carry],
        input_output_aliases={1 + len(after) + k: made + k for k in range(len(carry))},
        compiler_params=pltpu.CompilerParams(
            dimension_semantics=("arbitrary",), vmem_limit_bytes=room * 1024 * 1024
        ),
        cost_estimate=pl.CostEstimate(flops=flops, bytes_accessed=20_000_000, transcendentals=0),
        name=name,
    )

    def run(span, *operands):
        results = inner(span, *after, *carry, *operands)
        return results[0] if single else results

    return run


def shape_of(shape, dtype=F32):
    return jax.ShapeDtypeStruct(shape, dtype)


def once(
    kernel, operands, out_shapes, scratch, flops, name, spaces=(), after=(), carry=(), room=56
):
    spaces = dict(spaces)
    shapes = [*out_shapes, *(shape_of(x.shape, x.dtype) for x in carry)]
    count, extra = len(operands), len(after) + len(carry)
    anywhere = pl.BlockSpec(memory_space=pl.ANY)

    def whole(shape):
        return pl.BlockSpec(shape, lambda j: (0,) * len(shape), pipeline_mode=pl.Buffered(1))

    def body(*refs):
        outs = refs[count + extra : count + extra + len(out_shapes)]
        kernel(*refs[:count], *outs, *refs[count + extra + len(shapes) :])

    results = pl.pallas_call(
        body,
        grid=(1,),
        in_specs=[
            pl.BlockSpec(memory_space=spaces[k]) if k in spaces else whole(x.shape)
            for k, x in enumerate(operands)
        ]
        + [anywhere] * extra,
        out_specs=[whole(x.shape) for x in out_shapes] + [anywhere] * len(carry),
        out_shape=shapes,
        scratch_shapes=scratch,
        input_output_aliases={
            count + len(after) + k: len(out_shapes) + k for k in range(len(carry))
        },
        compiler_params=pltpu.CompilerParams(vmem_limit_bytes=room * 1024 * 1024),
        cost_estimate=pl.CostEstimate(flops=flops, bytes_accessed=5_000_000, transcendentals=0),
        name=name,
    )(*operands, *after, *carry)
    return results


def on_device(
    tokens,
    positions,
    item_of_atom,
    item_lengths,
    atom_types,
    key_mask,
    ln1_gain,
    ln1_bias,
    w_qkv,
    kernel_means,
    kernel_widths,
    kernel_weight,
    type_scale,
    type_shift,
    w_out,
    ln2_gain,
    ln2_bias,
    w_up,
    w_down,
    out_cotangent,
):
    own_rows, model_width = tokens.shape
    assert own_rows == LANES
    kernels, heads = kernel_weight.shape
    head_size = model_width // heads
    head_scale = head_size ** (-0.5)
    scale2 = head_scale * LOG2E
    groups = heads // GROUP
    width = groups * SPAN
    ff_width = w_up.shape[1]
    ka_count = lax.axis_size("ka")
    flat = lax.axis_index("pb") * ka_count + lax.axis_index("ka")
    flat_array = flat.astype(jnp.int32).reshape(1)
    reach = (PROT_LEN + own_rows - 2) // own_rows
    chips = (reach + 1) // 2
    pairs = 2 * chips + 1
    assert pairs == len(SLOTS[0])
    keys = 2 * own_rows
    atoms = positions.shape[1]
    atoms_blocks = atoms // LANES
    types = type_scale.shape[0]
    bits = bits_of("ka") - 1
    up_order = [(0, 1), (1, 2)] + [(bit, 1) for bit in range(3, bits)]
    rest_order = [(bit, 1) for bit in range(bits)]

    window = Window(tokens)
    cotangent_came = core_flip(out_cotangent)
    ln1 = [x.reshape(-1, LANES) for x in (ln1_gain, ln1_bias)]
    ln2 = [x.reshape(-1, LANES) for x in (ln2_gain, ln2_bias)]
    (normed_own,) = once(
        normal_kernel,
        (tokens, *ln1),
        [shape_of(tokens.shape, BF)],
        [],
        1_000_000,
        "first_normal",
        room=16,
    )
    gathered = Gathered(normed_own)

    select = select_table(head_size)
    place = place_table(heads, head_size)
    into_tail, out_of_tail = tail_tables(heads, head_size)
    type_tiles = -(-types // LANES)
    tables = jnp.pad(
        jnp.stack([type_scale, type_shift]), ((0, 0), (0, type_tiles * LANES - types))
    )
    tables = tables.reshape(2, type_tiles, LANES).swapaxes(0, 1).reshape(2 * type_tiles, LANES)
    lengths = jnp.pad(item_lengths, (0, -item_lengths.shape[0] % LANES)).reshape(-1, LANES)
    span, other, own, own_line, tabs, grad_weights, weights_turned, par = once(
        functools.partial(side_kernel, atoms_blocks),
        (
            flat_array,
            positions,
            item_of_atom.reshape(-1, LANES),
            key_mask.reshape(-1, LANES),
            atom_types.reshape(-1, LANES),
            lengths,
            tables,
            kernel_means.reshape(1, LANES),
            kernel_widths.reshape(1, LANES),
            kernel_weight.T,
        ),
        [
            shape_of((SPAN_ROWS, LANES), jnp.int32),
            shape_of((SIDE, pairs * keys)),
            shape_of((own_rows, LANES)),
            shape_of((SIDE, LANES)),
            shape_of((4, kernels, LANES)),
            shape_of((kernels, WEIGHT_PIECES * heads), BF),
            shape_of((heads, kernels), BF),
            shape_of((LANES, LANES)),
        ],
        [],
        1_000_000_000,
        "sides",
        {0: pltpu.SMEM},
    )

    own_spec = fixed((own_rows, LANES))
    other_spec = moving((SIDE, keys), 1)
    bias_spec = moving((1, own_rows, heads, keys))
    bias = call(
        bias_kernel,
        pairs,
        [own_spec, other_spec, fixed((4, kernels, LANES)), fixed((heads, kernels))],
        bias_spec,
        shape_of((pairs, own_rows, heads, keys)),
        [pltpu.VMEM((own_rows, keys), F32)],
        30_000_000_000,
        "pair_bias",
        after=(window.one, window.two, normed_own),
    )(span, own, other, tabs, weights_turned)
    window.middle()
    token_blocks = window.finish()

    expanded = pltpu.VMEM((groups, own_rows * GROUP, SPAN), BF)
    summed = pltpu.VMEM((groups, own_rows * GROUP, SPAN), F32)
    mask_scratch = pltpu.VMEM((own_rows, GROUP, keys), F32)
    line_scratch = pltpu.VMEM((groups, own_rows * GROUP, LANES), F32)
    attended, q_aug, lse_pieces, kvq = call(
        functools.partial(forward_kernel, scale2, groups),
        pairs,
        [own_spec, other_spec]
        + [fixed((own_rows, model_width))] * 14
        + [
            fixed((model_width // LANES, LANES)),
            fixed((model_width // LANES, LANES)),
            fixed((model_width, 3 * model_width)),
            fixed(select.shape),
            fixed((1, width)),
            fixed(place.shape),
            bias_spec,
        ],
        [
            fixed((own_rows, width)),
            fixed((own_rows, width)),
            fixed((PIECES, own_rows, LANES)),
            moving((1, keys, 3 * width)),
        ],
        [
            shape_of((own_rows, width)),
            shape_of((own_rows, width), BF),
            shape_of((PIECES, own_rows, LANES), BF),
            shape_of((pairs, keys, 3 * width), BF),
        ],
        [
            expanded,
            mask_scratch,
            line_scratch,
            line_scratch,
            summed,
            pltpu.VMEM((own_rows, LANES), F32),
            pltpu.VMEM((keys, model_width), BF),
        ],
        25_000_000_000,
        "attention_forward",
        after=(gathered.beside,),
    )(
        span,
        own,
        other,
        *token_blocks,
        *ln1,
        w_qkv,
        select,
        ones_row(heads, head_size),
        place,
        bias,
    )

    far_rows = gathered.far()
    tile = 3 * LANES
    assert ff_width % tile == 0 and tile % (2 * ff_width // ka_count) == 0
    row_shape = shape_of((own_rows, model_width), BF)
    slices = ka_count // 2
    up_rows, out_rows = ff_width // ka_count, model_width // ka_count
    pieces = shape_of((2, slices, up_rows, own_rows), BF)
    block_out, grad_mixed, do_aug, payload, attended_low, normed_second, *parts, ln2_grads = once(
        functools.partial(middle_kernel, groups, tile),
        (
            flat_array,
            tokens,
            attended,
            lse_pieces,
            *ln2,
            out_cotangent,
            w_out,
            w_up,
            w_down,
            select,
            place,
            head_sum_table(heads),
            into_tail,
        ),
        [
            row_shape,
            shape_of((own_rows, model_width)),
            shape_of((own_rows, width), BF),
            shape_of((own_rows, model_width + 2 * LANES), BF),
            row_shape,
            row_shape,
            pieces,
            pieces,
            shape_of((2, model_width)),
        ],
        [
            pltpu.VMEM((model_width, model_width), BF),
            pltpu.VMEM((model_width, ff_width), BF),
            pltpu.VMEM((ff_width, model_width), BF),
            pltpu.VMEM((own_rows, model_width), F32),
            pltpu.VMEM((own_rows, model_width), F32),
            pltpu.SemaphoreType.DMA,
            pltpu.SemaphoreType.DMA((2, ff_width // tile)),
        ],
        10_000_000_000,
        "feed_forward",
        {0: pltpu.SMEM, 7: pl.ANY, 8: pl.ANY, 9: pl.ANY},
        after=tuple(far_rows),
    )
    came = [core_flip(x) for x in (parts[1], normed_second, attended_low, payload)]
    window = Window(payload, came[3])
    gathered.finish()
    half = model_width // 2
    up_kept, up_sent, rest_kept, rest_sent = once(
        functools.partial(weight_grads_kernel, ka_count),
        (
            flat_array,
            parts[0],
            came[0],
            normed_second,
            came[1],
            out_cotangent,
            cotangent_came,
            attended_low,
            came[2],
            payload,
            came[3],
        ),
        [shape_of((slices // 2, up_rows, model_width), BF)] * 2
        + [shape_of((slices, up_rows + out_rows, half), BF)] * 2,
        [pltpu.VMEM((model_width, model_width), F32)],
        5_000_000_000,
        "weight_gradients",
        {0: pltpu.SMEM},
    )
    up_sum = slices_sum(up_kept, up_sent, up_order)
    rest_sum = columns_sum(rest_kept, rest_sent, rest_order)

    dq, grad_scores, window.one, window.two = call(
        functools.partial(query_grad_kernel, scale2, head_scale, groups),
        pairs,
        [
            own_spec,
            other_spec,
            fixed((own_rows, width)),
            fixed((own_rows, width)),
            moving((1, keys, 2 * width)),
            bias_spec,
            fixed(select.shape),
        ],
        [fixed((model_width, own_rows)), moving((1, own_rows, heads, keys))],
        [
            shape_of((model_width, own_rows), BF),
            shape_of((pairs, own_rows, heads, keys), BF),
        ],
        [expanded, expanded, mask_scratch, summed, pltpu.VMEM((own_rows, width), BF)],
        22_000_000_000,
        "query_gradients",
        after=(*up_sum.sent, *rest_sum.sent, window.far),
        carry=(window.one, window.two),
    )(span, own, other, q_aug, do_aug, kvq, bias, select)

    pos_blocks = atoms_blocks + 4 * chips
    small, pos_part = call(
        functools.partial(phi_grad_kernel, 0),
        pairs,
        [
            own_spec,
            other_spec,
            fixed((SIDE, LANES)),
            moving((1, own_rows, heads, keys)),
            fixed((4, kernels, LANES)),
            fixed((kernels, WEIGHT_PIECES * heads)),
            fixed((LANES, LANES)),
        ],
        [fixed((LANES, LANES)), fixed((3 * pos_blocks, LANES))],
        [shape_of((LANES, LANES)), shape_of((3 * pos_blocks, LANES))],
        [
            pltpu.VMEM((own_rows, keys), F32),
            pltpu.VMEM((own_rows, keys), F32),
            pltpu.VMEM((5, own_rows, LANES), F32),
            pltpu.VMEM((kernels, heads), F32),
            pltpu.VMEM((2, kernels, LANES), F32),
            pltpu.VMEM((2, 2 * LANES, LANES), F32),
        ],
        40_000_000_000,
        "kernel_gradients",
    )(span, own, other, own_line, grad_scores, tabs, grad_weights, par)
    window.middle()
    payload_blocks = window.finish()
    early_sum = everywhere_sum(
        jnp.concatenate([small, ln2_grads.reshape(-1, LANES), pos_part], axis=0)
    )
    advance([up_sum, rest_sum, early_sum], flat_array, "sums_first", (small,))

    dkv = call(
        functools.partial(key_grad_kernel, scale2, head_scale, groups, model_width),
        pairs,
        [
            own_spec,
            other_spec,
            pl.BlockSpec(
                (1, own_rows, 2 * width),
                lambda j, span: (chips, span[SPAN_CORE, 0], 0),
                pipeline_mode=pl.Buffered(1),
            ),
            moving((1, keys, width), 0, 2),
        ]
        + [fixed((own_rows, model_width + 2 * LANES))] * 14
        + [
            fixed((model_width, model_width)),
            fixed(select.shape),
            fixed(out_of_tail.shape),
            bias_spec,
        ],
        fixed((2 * model_width, own_rows)),
        shape_of((2 * model_width, own_rows), BF),
        [
            expanded,
            expanded,
            mask_scratch,
            pltpu.VMEM((keys, width), BF),
            pltpu.VMEM((keys, width), BF),
            summed,
            summed,
            pltpu.VMEM((keys, model_width + 2 * LANES), BF),
            pltpu.VMEM((2, own_rows, width), BF),
        ],
        28_000_000_000,
        "key_gradients",
        after=(*up_sum.sent, *rest_sum.sent, *early_sum.sent),
    )(span, own, other, kvq, kvq, *payload_blocks, w_out, select, out_of_tail, bias)

    advance([up_sum, rest_sum, early_sum], flat_array, "sums_second", (dkv,))
    qkv_rows = 3 * model_width // ka_count
    norm_count = model_width // LANES
    sent_rows = qkv_rows + -(-2 * norm_count // 16) * 16
    part_shape = shape_of((ka_count // 4, sent_rows, own_rows), BF)
    grad_tokens, stay, to_core, to_chip, to_both = once(
        functools.partial(first_norm_kernel, ka_count),
        (flat_array, tokens, ln1[0], dq, dkv, w_qkv, grad_mixed),
        [shape_of((own_rows, model_width))] + [part_shape] * 4,
        [pltpu.VMEM((3 * model_width, own_rows), BF)],
        2_000_000_000,
        "first_norm",
        {0: pltpu.SMEM},
        after=tuple(early_sum.sent),
        room=24,
    )
    core_stay, core_go = core_flip(to_core), core_flip(to_both)
    chip_own, chip_core = flip_bit(to_chip, "ka", 1), flip_bit(core_go, "ka", 1)
    groups_out = once(
        regroup_kernel,
        (stay, core_stay, chip_own, chip_core),
        [shape_of((4, sent_rows, own_rows), BF)] * (ka_count // 4),
        [],
        1_000_000,
        "regroup",
        room=24,
    )
    advance([up_sum, rest_sum, early_sum], flat_array, "sums_third", (groups_out[0],))
    groups_in = [groups_out[0]] + [
        flip_mask(groups_out[i], "ka", 4 * i) for i in range(1, ka_count // 4)
    ]
    qkv_part, norm_part = once(
        functools.partial(qkv_grads_kernel, gathered.masks(), ka_count // 4),
        (*groups_in, *gathered.arrays()),
        [shape_of((qkv_rows, model_width), BF), shape_of((sent_rows - qkv_rows, LANES))],
        [],
        3_000_000_000,
        "qkv_gradients",
    )
    qkv_sum = Sum(qkv_part, [qkv_part], over("pb"))
    norm_sum = Sum(norm_part, [norm_part], over("pb"))
    advance([up_sum, rest_sum, early_sum], flat_array, "sums_fourth", (qkv_part,))
    sums = [qkv_sum, norm_sum, up_sum, rest_sum, early_sum]
    while any(one.stages for one in sums):
        advance(sums, flat_array, "sums_last")
    joined = early_sum.total
    up_total, rest_total = up_sum.total, rest_sum.total
    norms, by_weight, by_mean, by_width, by_scale, by_shift, grad_positions = once(
        functools.partial(results_kernel, heads, types),
        (flat_array, joined, norm_sum.total),
        [
            shape_of((4, norm_count, LANES)),
            shape_of((kernels, heads)),
            shape_of((1, kernels)),
            shape_of((1, kernels)),
            shape_of((1, types)),
            shape_of((1, types)),
            shape_of((3, LANES)),
        ],
        [],
        1_000_000,
        "results",
        {0: pltpu.SMEM},
        room=16,
    )
    qkv_total = qkv_sum.total
    return (
        block_out,
        grad_tokens,
        grad_positions,
        norms[0].reshape(-1),
        norms[1].reshape(-1),
        qkv_total.T,
        by_mean.reshape(-1),
        by_width.reshape(-1),
        by_weight,
        by_scale.reshape(-1),
        by_shift.reshape(-1),
        rest_total[up_rows:].T,
        norms[2].reshape(-1),
        norms[3].reshape(-1),
        up_total.T,
        rest_total[:up_rows],
    )


def solution(mesh):
    rows = P(MESH, None)
    in_specs = (rows,) + (P(),) * 18 + (rows,)
    out_specs = (
        rows,
        rows,
        P(None, MESH),
        P(),
        P(),
        P(None, "ka"),
        P(),
        P(),
        P(),
        P(),
        P(),
        P(None, "ka"),
        P(),
        P(),
        P(None, "ka"),
        P("ka", None),
    )
    return jax.shard_map(
        on_device, mesh=mesh, in_specs=in_specs, out_specs=out_specs, check_vma=False
    )
```

profile of v0, /device:TPU:0, one launch (start us, length us, event | category | flops | bytes accessed | tf_op | source)
XLA Modules:
  0.0 307.9 jit_solution(4561678879772341904)
XLA Ops:
  19.0 7.1 %collective-permute-done.4.refs_7_ = bf16[128,768]{1,0:T(8,128)(2,1)S(1)} collective-permute-done((bf16[128,768]{1,0:T(8,128)(2,1)}, bf16[128,768]{1,0:T(8,128)(2,1)S(1)}, u32[]{:S(2)}, u32[]{:S(2)}) %collective-permute-start.4) | collective-permute-done | bytes 196640 | tf_op jit(solution)/shard_map/ppermute | solution.py:130
  28.7 6.4 %sides.1 = (s32[48,128]{1,0:T(8,128)}, f32[16,1792]{1,0:T(8,128)}, f32[128,128]{1,0:T(8,128)}, f32[16,128]{1,0:T(8,128)}, f32[4,128,128]{2,1,0:T(8,128)}, /*inde...) custom-call(s32[1]{0:T(128)} %bitcast.refs_0_, f32[3,4096]{1,0:T(4,128)} %refs_1_.3, ...), custom_call_target="tpu_custom_call" | custom-call | flops 1000000000 | bytes 5000000 | tf_op jit(solution)/shard_map/sides/pallas_call | solution.py:1403
  36.4 7.9 %pair_bias.1.refs_23_.refs_10_.refs_26_ = f32[7,128,32,256]{3,2,1,0:T(8,128)} custom-call(s32[48,128]{1,0:T(8,128)} %get-tuple-element.86.span_ref, bf16[128,768]{1,0:T(8,128)(2,1)} %copy-done.45, bf16[128,768]{1,0:T(8,128)(2,1)} %copy-done.46, bf16[128,768]{1,0:T(8,128)(2,1)} %copy-done.2, f32[128,128]{1,0:T(8,128)} %get-tuple-element.87.refs_3_.refs_1_.refs_5_.refs_0_, ...), custom_call_target="tpu_custom_call" | custom-call | flops 30000001024 | bytes 20000000 | tf_op jit(solution)/shard_map/pair_bias/pallas_call | solution.py:1378
  50.2 17.1 %attention_forward.1 = (f32[128,1024]{1,0:T(8,128)}, bf16[128,1024]{1,0:T(8,128)(2,1)}, bf16[3,128,128]{2,1,0:T(8,128)(2,1)}, bf16[7,256,3072]{2,1,0:T(8,128)(2,1)}) custom-call(s32[48,128]{1,0:T(8,128)} %get-tuple-element.86.span_ref, bf16[128,768]{1,0:T(8,128)(2,1)} %copy-done.22, f32[128,128]{1,0:T(8,128)} %get-tuple-element.87.refs_3_.refs_1_.refs_5_.refs_0_, ...), custom_call_target="tpu_custom_call" | custom-call | flops 24999999488 | bytes 20000000 | tf_op jit(solution)/shard_map/attention_forward/pallas_call | solution.py:1378
  67.4 8.1 %collective-permute-done.15.refs_15_.refs_9_ = bf16[2,128,768]{2,1,0:T(8,128)(2,1)S(1)} collective-permute-done((bf16[2,128,768]{2,1,0:T(8,128)(2,1)S(1)}, bf16[2,128,768]{2,1,0:T(8,128)(2,1)S(1)}, u32[]{:S(2)}, u32[]{:S(2)}) %collective-permute-start.15) | collective-permute-done | bytes 393248 | tf_op jit(solution)/shard_map/ppermute | solution.py:139
  76.3 19.3 %feed_forward.1 = (bf16[128,768]{1,0:T(8,128)(2,1)}, f32[128,768]{1,0:T(8,128)}, bf16[128,1024]{1,0:T(8,128)(2,1)}, bf16[128,1024]{1,0:T(8,128)(2,1)}, bf16[128,...) custom-call(s32[1]{0:T(128)} %bitcast.refs_0_, ...), custom_call_target="tpu_custom_call" | custom-call | flops 10000000000 | bytes 5000000 | tf_op jit(solution)/shard_map/feed_forward/pallas_call | solution.py:1403
  96.3 19.1 %collective-permute-start.22 = (bf16[128,1024]{1,0:T(8,128)(2,1)}, bf16[128,1024]{1,0:T(8,128)(2,1)S(1)}, u32[]{:S(2)}, u32[]{:S(2)}) collective-permute-start(bf16[128,1024]{1,0:T(8,128)(2,1)} %get-tuple-element.98.refs_9_.refs_12_), channel_id=1, source_target_pairs={{0,26},{1,27},{2,8},{3,9},{4,30},{5,31},{6,12},{7,13},{8,2},{9,3},... | collective-permute-start | bytes 786440 | tf_op jit(solution)/shard_map/ppermute | solution.py:68
  123.7 9.9 %weight_gradients.1 = (bf16[4,192,768]{2,1,0:T(8,128)(2,1)}, bf16[4,192,768]{2,1,0:T(8,128)(2,1)}, bf16[8,240,384]{2,1,0:T(8,128)(2,1)}, bf16[8,240,384]{2,1,0:T(8,128)(2,1)}) custom-call(s32[1]{0:T(128)} %bitcast.refs_0_, bf16[2,8,192,128]{3,2,1,0:T(8,128)(2,1)} %get-tuple-element.94.refs_1_, bf16[2,8,192,128]{3,2,1,0:T(8,128)(2,1)} %copy-done.24, ...), custom_call_target="tpu_custom_call" | custom-call | flops 5000000000 | bytes 5000000 | tf_op jit(solution)/shard_map/weight_gradients/pallas_call | solution.py:1403
  133.6 11.1 %collective-permute-start.26 = (bf16[8,240,384]{2,1,0:T(8,128)(2,1)}, bf16[8,240,384]{2,1,0:T(8,128)(2,1)S(1)}, u32[]{:S(2)}, u32[]{:S(2)}) collective-permute-start(bf16[8,240,384]{2,1,0:T(8,128)(2,1)} %get-tuple-element.100.refs_1_), channel_id=1, source_target_pairs={{0,16},{16,0},{1,17},{17,1},{2,18},{18,2},{3,19},{19,3},{4,20},{20... | collective-permute-start | bytes 4423688 | tf_op jit(solution)/shard_map/ppermute | solution.py:139
  144.7 11.6 %query_gradients.1 = (bf16[768,128]{1,0:T(8,128)(2,1)}, bf16[7,128,32,256]{3,2,1,0:T(8,128)(2,1)}, bf16[128,1024]{1,0:T(8,128)(2,1)}, bf16[128,1024]{1,0:T(8,128)(2,1)}) custom-call(s32[48,128]{1,0:T(8,128)} %get-tuple-element.86.span_ref, bf16[4,192,768]{2,1,0:T(8,128)(2,1)} %get-tuple-element.99.refs_0_, ...), custom_call_target="tpu_custom_call", output_to_operand_aliasing={{2}: (4, {}), {3}: (5, {})} | custom-call | flops 22000001024 | bytes 20000000 | tf_op jit(solution)/shard_map/query_gradients/pallas_call | solution.py:1378
  156.3 3.8 %collective-permute-start.28 = (bf16[128,1024]{1,0:T(8,128)(2,1)}, bf16[128,1024]{1,0:T(8,128)(2,1)}, u32[]{:S(2)}, u32[]{:S(2)}) collective-permute-start(bf16[128,1024]{1,0:T(8,128)(2,1)} %get-tuple-element.119.refs_10_), channel_id=1, source_target_pairs={{0,2},{1,3},{2,0},{3,1},{4,6},{5,7},{6,4},{7,5},{8,10},{9,11},{10,... | collective-permute-start | bytes 786440 | tf_op jit(solution)/shard_map/ppermute | solution.py:130
  160.2 10.5 %kernel_gradients.1 = (f32[128,128]{1,0:T(8,128)}, f32[132,128]{1,0:T(8,128)}) custom-call(s32[48,128]{1,0:T(8,128)} %get-tuple-element.86.span_ref, f32[128,128]{1,0:T(8,128)} %get-tuple-element.87.refs_3_.refs_1_.refs_5_.refs_0_, f32[16,1792]{1,0:T(8,128)} %get-tuple-element.88.refs_4_.refs_2_.refs_6_.refs_1_, f32[16,128]{1,0:T(8,128)} %get-tuple-element.107.refs_2_, ...), custom_call_target="tpu_custom_call" | custom-call | flops 40000000000 | bytes 20000000 | tf_op jit(solution)/shard_map/kernel_gradients/pallas_call | solution.py:1378
  174.1 5.4 %collective-permute-done.28.refs_11_ = bf16[128,1024]{1,0:T(8,128)(2,1)} collective-permute-done((bf16[128,1024]{1,0:T(8,128)(2,1)}, bf16[128,1024]{1,0:T(8,128)(2,1)}, u32[]{:S(2)}, u32[]{:S(2)}) %collective-permute-start.28) | collective-permute-done | bytes 262176 | tf_op jit(solution)/shard_map/ppermute | solution.py:130
  179.5 4.9 %collective-permute-done.30.refs_15_ = bf16[128,1024]{1,0:T(8,128)(2,1)} collective-permute-done((bf16[128,1024]{1,0:T(8,128)(2,1)}, bf16[128,1024]{1,0:T(8,128)(2,1)}, u32[]{:S(2)}, u32[]{:S(2)}) %collective-permute-start.30) | collective-permute-done | bytes 262176 | tf_op jit(solution)/shard_map/ppermute | solution.py:130
  187.3 3.9 %collective-permute-start.39 = (bf16[1,192,768]{2,1,0:T(8,128)(2,1)S(1)}, bf16[1,192,768]{2,1,0:T(8,128)(2,1)S(1)}, u32[]{:S(2)}, u32[]{:S(2)}) collective-permute-start(bf16[1,192,768]{2,1,0:T(8,128)(2,1)S(1)} %get-tuple-element.116.refs_2_), channel_id=1, source_target_pairs={{0,12},{1,13},{2,14},{3,15},{4,8},{5,9},{6,10},{7,11},{8,4},{9,5},... | collective-permute-start | bytes 884744 | tf_op jit(solution)/shard_map/ppermute | solution.py:139
  193.8 15.4 %key_gradients.1.refs_9_.refs_4_ = bf16[1536,128]{1,0:T(8,128)(2,1)} custom-call(s32[48,128]{1,0:T(8,128)} %get-tuple-element.86.span_ref, bf16[1,192,768]{2,1,0:T(8,128)(2,1)} %copy-done.12, bf16[1,192,768]{2,1,0:T(8,128)(2,1)} %copy-done.11, bf16[1,192,768]{2,1,0:T(8,128)(2,1)} %copy-done.10, bf16[4,240,384]{2,1,0:T(8,128)(2,1)} %copy-done.9, ...), custom_call_target="tpu_custom_call" | custom-call | flops 28000000000 | bytes 20000000 | tf_op jit(solution)/shard_map/key_gradients/pallas_call | solution.py:1378
  216.4 3.6 %first_norm.1 = (f32[128,768]{1,0:T(8,128)}, bf16[4,160,128]{2,1,0:T(8,128)(2,1)S(1)}, bf16[4,160,128]{2,1,0:T(8,128)(2,1)S(1)}, bf16[4,160,128]{2,1,0:T(8,128)(2,1)S(1)}, bf16[4,160,128]{2,1,0:T(8,128)(2,1)S(1)}) custom-call(s32[1]{0:T(128)} %bitcast.refs_0_, bf16[128,768]{1,0:T(8,128)(2,1)} %refs_1_.5, f32[6,128]{1,0:T(8,128)S(1)} %bitcast.48, ...), custom_call_target="tpu_custom_call" | custom-call | flops 2000000000 | bytes 5000000 | tf_op jit(solution)/shard_map/first_norm/pallas_call | solution.py:1403
  221.9 5.4 %collective-permute-start.55 = (bf16[2,240,384]{2,1,0:T(8,128)(2,1)S(1)}, bf16[2,240,384]{2,1,0:T(8,128)(2,1)S(1)}, u32[]{:S(2)}, u32[]{:S(2)}) collective-permute-start(bf16[2,240,384]{2,1,0:T(8,128)(2,1)S(1)} %get-tuple-element.138), channel_id=1, source_target_pairs={{0,4},{1,5},{2,6},{3,7},{4,0},{5,1},{6,2},{7,3},{8,12},{9,13},{10,... | collective-permute-start | bytes 1105928 | tf_op jit(solution)/shard_map/ppermute | solution.py:139
  227.7 24.3 %collective-permute-start.54 = (bf16[192,768]{1,0:T(8,128)(2,1)S(1)}, bf16[192,768]{1,0:T(8,128)(2,1)S(1)}, u32[]{:S(2)}, u32[]{:S(2)}) collective-permute-start(bf16[192,768]{1,0:T(8,128)(2,1)S(1)} %bitcast.49), channel_id=1, source_target_pairs={{0,16},{16,0},{1,17},{17,1},{2,18},{18,2},{3,19},{19,3},{4,20},{20... | collective-permute-start | bytes 884744 | tf_op jit(solution)/shard_map/ppermute | solution.py:139
  253.7 4.4 %collective-permute-done.56.refs_6_ = f32[272,128]{1,0:T(8,128)S(1)} collective-permute-done((f32[272,128]{1,0:T(8,128)S(1)}, f32[272,128]{1,0:T(8,128)S(1)}, u32[]{:S(2)}, u32[]{:S(2)}) %collective-permute-start.56) | collective-permute-done | bytes 139296 | tf_op jit(solution)/shard_map/ppermute | solution.py:139
  266.5 13.5 %collective-permute-done.47.refs_2_ = bf16[4,160,128]{2,1,0:T(8,128)(2,1)S(1)} collective-permute-done((bf16[4,160,128]{2,1,0:T(8,128)(2,1)S(1)}, bf16[4,160,128]{2,1,0:T(8,128)(2,1)S(1)}, u32[]{:S(2)}, u32[]{:S(2)}) %collective-permute-start.47) | collective-permute-done | bytes 163872 | tf_op jit(solution)/shard_map/ppermute | solution.py:139
  284.2 6.0 %collective-permute-start.59 = (bf16[144,768]{1,0:T(8,128)(2,1)}, bf16[144,768]{1,0:T(8,128)(2,1)S(1)}, u32[]{:S(2)}, u32[]{:S(2)}) collective-permute-start(bf16[144,768]{1,0:T(8,128)(2,1)} %get-tuple-element.134.refs_5_.refs_1_), channel_id=1, source_target_pairs={{0,16},{16,0},{1,17},{17,1},{2,18},{18,2},{3,19},{19,3},{4,20},{20... | collective-permute-start | bytes 663560 | tf_op jit(solution)/shard_map/ppermute | solution.py:139
  291.2 5.3 %collective-permute-start.61 = (bf16[240,384]{1,0:T(8,128)(2,1)S(1)}, bf16[240,384]{1,0:T(8,128)(2,1)S(1)}, u32[]{:S(2)}, u32[]{:S(2)}) collective-permute-start(bf16[240,384]{1,0:T(8,128)(2,1)S(1)} %bitcast.51), channel_id=1, source_target_pairs={{0,16},{16,0},{1,17},{17,1},{2,18},{18,2},{3,19},{19,3},{4,20},{20... | collective-permute-start | bytes 552968 | tf_op jit(solution)/shard_map/ppermute | solution.py:139
  298.5 5.0 %collective-permute-done.60.refs_6_ = f32[16,128]{1,0:T(8,128)S(1)} collective-permute-done((f32[16,128]{1,0:T(8,128)S(1)}, f32[16,128]{1,0:T(8,128)S(1)}, u32[]{:S(2)}, u32[]{:S(2)}) %collective-permute-start.60) | collective-permute-done | bytes 8224 | tf_op jit(solution)/shard_map/ppermute | solution.py:139
  (257 shorter events, 77.7 us)
Async XLA Ops:
  11.8 23.3 %collective-permute-start.1 = (bf16[128,768]{1,0:T(8,128)(2,1)}, bf16[128,768]{1,0:T(8,128)(2,1)S(1)}, u32[]{:S(2)}, u32[]{:S(2)}) collective-permute-start(bf16[128,768]{1,0:T(8,128)(2,1)} %refs_1_.5), channel_id=1, source_target_pairs={{0,26},{1,27},{2,8},{3,9},{4,30},{5,31},{6,12},{7,13},{8,2},{9,3},... | collective-permute-start | bytes 589832 | tf_op jit(solution)/shard_map/ppermute | solution.py:68
  45.7 29.8 %collective-permute-start.15 = (bf16[2,128,768]{2,1,0:T(8,128)(2,1)S(1)}, bf16[2,128,768]{2,1,0:T(8,128)(2,1)S(1)}, u32[]{:S(2)}, u32[]{:S(2)}) collective-permute-start(bf16[2,128,768]{2,1,0:T(8,128)(2,1)S(1)} %pad_maximum_fusion), channel_id=1, source_target_pairs={{0,8},{1,9},{2,10},{3,11},{4,12},{5,13},{6,14},{7,15},{8,0},{9,1},... | collective-permute-start | bytes 1179656 | tf_op jit(solution)/shard_map/ppermute | solution.py:139
  45.7 29.7 %collective-permute-start.16 = (bf16[2,128,768]{2,1,0:T(8,128)(2,1)S(1)}, bf16[2,128,768]{2,1,0:T(8,128)(2,1)S(1)}, u32[]{:S(2)}, u32[]{:S(2)}) collective-permute-start(bf16[2,128,768]{2,1,0:T(8,128)(2,1)S(1)} %pad_maximum_fusion), channel_id=1, source_target_pairs={{0,12},{1,13},{2,14},{3,15},{4,8},{5,9},{6,10},{7,11},{8,4},{9,5},... | collective-permute-start | bytes 1179656 | tf_op jit(solution)/shard_map/ppermute | solution.py:139
  95.6 27.2 %collective-permute-start.17 = (bf16[2,8,192,128]{3,2,1,0:T(8,128)(2,1)}, bf16[2,8,192,128]{3,2,1,0:T(8,128)(2,1)S(1)}, u32[]{:S(2)}, u32[]{:S(2)}) collective-permute-start(bf16[2,8,192,128]{3,2,1,0:T(8,128)(2,1)} %get-tuple-element.95), channel_id=1, source_target_pairs={{0,1},{1,0},{2,3},{3,2},{4,5},{5,4},{6,7},{7,6},{8,9},{9,8},{10,11... | collective-permute-start | bytes 2359304 | tf_op jit(solution)/shard_map/ppermute | solution.py:47
  96.2 24.7 %collective-permute-start.21 = (bf16[128,1024]{1,0:T(8,128)(2,1)}, bf16[128,1024]{1,0:T(8,128)(2,1)S(1)}, u32[]{:S(2)}, u32[]{:S(2)}) collective-permute-start(bf16[128,1024]{1,0:T(8,128)(2,1)} %get-tuple-element.98.refs_9_.refs_12_), channel_id=1, source_target_pairs={{0,1},{1,0},{2,3},{3,2},{4,5},{5,4},{6,7},{7,6},{8,9},{9,8},{10,11... | collective-permute-start | bytes 786440 | tf_op jit(solution)/shard_map/ppermute | solution.py:47
  96.3 26.4 %collective-permute-start.22 = (bf16[128,1024]{1,0:T(8,128)(2,1)}, bf16[128,1024]{1,0:T(8,128)(2,1)S(1)}, u32[]{:S(2)}, u32[]{:S(2)}) collective-permute-start(bf16[128,1024]{1,0:T(8,128)(2,1)} %get-tuple-element.98.refs_9_.refs_12_), channel_id=1, source_target_pairs={{0,26},{1,27},{2,8},{3,9},{4,30},{5,31},{6,12},{7,13},{8,2},{9,3},... | collective-permute-start | bytes 786440 | tf_op jit(solution)/shard_map/ppermute | solution.py:68
  117.1 27.7 %collective-permute-start.23 = (bf16[128,1024]{1,0:T(8,128)(2,1)}, bf16[128,1024]{1,0:T(8,128)(2,1)}, u32[]{:S(2)}, u32[]{:S(2)}) collective-permute-start(bf16[128,1024]{1,0:T(8,128)(2,1)} %get-tuple-element.98.refs_9_.refs_12_), channel_id=1, source_target_pairs={{0,4},{1,5},{2,6},{3,7},{4,0},{5,1},{6,2},{7,3},{8,12},{9,13},{10,... | collective-permute-start | bytes 786440 | tf_op jit(solution)/shard_map/ppermute | solution.py:66
  117.3 27.4 %collective-permute-start.24 = (bf16[128,1024]{1,0:T(8,128)(2,1)}, bf16[128,1024]{1,0:T(8,128)(2,1)}, u32[]{:S(2)}, u32[]{:S(2)}) collective-permute-start(bf16[128,1024]{1,0:T(8,128)(2,1)} %get-tuple-element.98.refs_9_.refs_12_), channel_id=1, source_target_pairs={{0,28},{1,29},{2,30},{3,31},{4,8},{5,9},{6,10},{7,11},{8,4},{9,5},... | collective-permute-start | bytes 786440 | tf_op jit(solution)/shard_map/ppermute | solution.py:67
  120.8 39.2 %collective-permute-start.29 = (bf16[128,1024]{1,0:T(8,128)(2,1)}, bf16[128,1024]{1,0:T(8,128)(2,1)}, u32[]{:S(2)}, u32[]{:S(2)}) collective-permute-start(bf16[128,1024]{1,0:T(8,128)(2,1)} %get-tuple-element.98.refs_9_.refs_12_), channel_id=1, source_target_pairs={{0,2},{1,3},{2,0},{3,1},{4,6},{5,7},{6,4},{7,5},{8,10},{9,11},{10,... | collective-permute-start | bytes 786440 | tf_op jit(solution)/shard_map/ppermute | solution.py:130
  122.8 48.8 %collective-permute-start.31 = (bf16[128,1024]{1,0:T(8,128)(2,1)S(1)}, bf16[128,1024]{1,0:T(8,128)(2,1)S(1)}, u32[]{:S(2)}, u32[]{:S(2)}) collective-permute-start(bf16[128,1024]{1,0:T(8,128)(2,1)S(1)} %collective-permute-done.22.refs_2_.refs_9_), channel_id=1, source_target_pairs={{0,1},{1,0},{2,3},{3,2},{4,5},{5,4},{6,7},{7,6},{8,9},{9,8},{10,11... | collective-permute-start | bytes 786440 | tf_op jit(solution)/shard_map/ppermute | solution.py:47
  133.6 51.2 %collective-permute-start.26 = (bf16[8,240,384]{2,1,0:T(8,128)(2,1)}, bf16[8,240,384]{2,1,0:T(8,128)(2,1)S(1)}, u32[]{:S(2)}, u32[]{:S(2)}) collective-permute-start(bf16[8,240,384]{2,1,0:T(8,128)(2,1)} %get-tuple-element.100.refs_1_), channel_id=1, source_target_pairs={{0,16},{16,0},{1,17},{17,1},{2,18},{18,2},{3,19},{19,3},{4,20},{20... | collective-permute-start | bytes 4423688 | tf_op jit(solution)/shard_map/ppermute | solution.py:139
  144.7 39.6 %collective-permute-start.25 = (bf16[4,192,768]{2,1,0:T(8,128)(2,1)}, bf16[4,192,768]{2,1,0:T(8,128)(2,1)S(1)}, u32[]{:S(2)}, u32[]{:S(2)}) collective-permute-start(bf16[4,192,768]{2,1,0:T(8,128)(2,1)} %get-tuple-element.99.refs_0_), channel_id=1, source_target_pairs={{0,2},{1,3},{2,0},{3,1},{4,6},{5,7},{6,4},{7,5},{8,10},{9,11},{10,... | collective-permute-start | bytes 3538952 | tf_op jit(solution)/shard_map/ppermute | solution.py:139
  160.1 24.3 %collective-permute-start.30 = (bf16[128,1024]{1,0:T(8,128)(2,1)}, bf16[128,1024]{1,0:T(8,128)(2,1)}, u32[]{:S(2)}, u32[]{:S(2)}) collective-permute-start(bf16[128,1024]{1,0:T(8,128)(2,1)} %get-tuple-element.120.refs_14_), channel_id=1, source_target_pairs={{0,2},{1,3},{2,0},{3,1},{4,6},{5,7},{6,4},{7,5},{8,10},{9,11},{10,... | collective-permute-start | bytes 786440 | tf_op jit(solution)/shard_map/ppermute | solution.py:130
  186.5 25.0 %collective-permute-start.40 = (bf16[4,240,384]{2,1,0:T(8,128)(2,1)S(1)}, bf16[4,240,384]{2,1,0:T(8,128)(2,1)S(1)}, u32[]{:S(2)}, u32[]{:S(2)}) collective-permute-start(bf16[4,240,384]{2,1,0:T(8,128)(2,1)S(1)} %get-tuple-element.117.refs_3_), channel_id=1, source_target_pairs={{0,2},{1,3},{2,0},{3,1},{4,6},{5,7},{6,4},{7,5},{8,10},{9,11},{10,... | collective-permute-start | bytes 2211848 | tf_op jit(solution)/shard_map/ppermute | solution.py:139
  186.8 24.1 %collective-permute-start.37 = (bf16[1,192,768]{2,1,0:T(8,128)(2,1)S(1)}, bf16[1,192,768]{2,1,0:T(8,128)(2,1)S(1)}, u32[]{:S(2)}, u32[]{:S(2)}) collective-permute-start(bf16[1,192,768]{2,1,0:T(8,128)(2,1)S(1)} %get-tuple-element.114.refs_0_), channel_id=1, source_target_pairs={{0,4},{1,5},{2,6},{3,7},{4,0},{5,1},{6,2},{7,3},{8,12},{9,13},{10,... | collective-permute-start | bytes 884744 | tf_op jit(solution)/shard_map/ppermute | solution.py:139
  186.9 24.2 %collective-permute-start.38 = (bf16[1,192,768]{2,1,0:T(8,128)(2,1)S(1)}, bf16[1,192,768]{2,1,0:T(8,128)(2,1)S(1)}, u32[]{:S(2)}, u32[]{:S(2)}) collective-permute-start(bf16[1,192,768]{2,1,0:T(8,128)(2,1)S(1)} %get-tuple-element.115.refs_1_), channel_id=1, source_target_pairs={{0,8},{1,9},{2,10},{3,11},{4,12},{5,13},{6,14},{7,15},{8,0},{9,1},... | collective-permute-start | bytes 884744 | tf_op jit(solution)/shard_map/ppermute | solution.py:139
  187.3 24.2 %collective-permute-start.39 = (bf16[1,192,768]{2,1,0:T(8,128)(2,1)S(1)}, bf16[1,192,768]{2,1,0:T(8,128)(2,1)S(1)}, u32[]{:S(2)}, u32[]{:S(2)}) collective-permute-start(bf16[1,192,768]{2,1,0:T(8,128)(2,1)S(1)} %get-tuple-element.116.refs_2_), channel_id=1, source_target_pairs={{0,12},{1,13},{2,14},{3,15},{4,8},{5,9},{6,10},{7,11},{8,4},{9,5},... | collective-permute-start | bytes 884744 | tf_op jit(solution)/shard_map/ppermute | solution.py:139
  220.1 31.8 %collective-permute-start.42 = (bf16[4,160,128]{2,1,0:T(8,128)(2,1)S(1)}, bf16[4,160,128]{2,1,0:T(8,128)(2,1)S(1)}, u32[]{:S(2)}, u32[]{:S(2)}) collective-permute-start(bf16[4,160,128]{2,1,0:T(8,128)(2,1)S(1)} %get-tuple-element.127), channel_id=1, source_target_pairs={{0,1},{1,0},{2,3},{3,2},{4,5},{5,4},{6,7},{7,6},{8,9},{9,8},{10,11... | collective-permute-start | bytes 491528 | tf_op jit(solution)/shard_map/ppermute | solution.py:47
  220.5 31.4 %collective-permute-start.43 = (bf16[4,160,128]{2,1,0:T(8,128)(2,1)S(1)}, bf16[4,160,128]{2,1,0:T(8,128)(2,1)S(1)}, u32[]{:S(2)}, u32[]{:S(2)}) collective-permute-start(bf16[4,160,128]{2,1,0:T(8,128)(2,1)S(1)} %get-tuple-element.128), channel_id=1, source_target_pairs={{0,2},{1,3},{2,0},{3,1},{4,6},{5,7},{6,4},{7,5},{8,10},{9,11},{10,... | collective-permute-start | bytes 491528 | tf_op jit(solution)/shard_map/ppermute | solution.py:130
  221.9 37.4 %collective-permute-start.55 = (bf16[2,240,384]{2,1,0:T(8,128)(2,1)S(1)}, bf16[2,240,384]{2,1,0:T(8,128)(2,1)S(1)}, u32[]{:S(2)}, u32[]{:S(2)}) collective-permute-start(bf16[2,240,384]{2,1,0:T(8,128)(2,1)S(1)} %get-tuple-element.138), channel_id=1, source_target_pairs={{0,4},{1,5},{2,6},{3,7},{4,0},{5,1},{6,2},{7,3},{8,12},{9,13},{10,... | collective-permute-start | bytes 1105928 | tf_op jit(solution)/shard_map/ppermute | solution.py:139
  227.3 25.2 %collective-permute-start.45 = (bf16[4,160,128]{2,1,0:T(8,128)(2,1)S(1)}, bf16[4,160,128]{2,1,0:T(8,128)(2,1)S(1)}, u32[]{:S(2)}, u32[]{:S(2)}) collective-permute-start(bf16[4,160,128]{2,1,0:T(8,128)(2,1)S(1)} %collective-permute-done.44), channel_id=1, source_target_pairs={{0,2},{1,3},{2,0},{3,1},{4,6},{5,7},{6,4},{7,5},{8,10},{9,11},{10,... | collective-permute-start | bytes 491528 | tf_op jit(solution)/shard_map/ppermute | solution.py:130
  227.7 31.6 %collective-permute-start.54 = (bf16[192,768]{1,0:T(8,128)(2,1)S(1)}, bf16[192,768]{1,0:T(8,128)(2,1)S(1)}, u32[]{:S(2)}, u32[]{:S(2)}) collective-permute-start(bf16[192,768]{1,0:T(8,128)(2,1)S(1)} %bitcast.49), channel_id=1, source_target_pairs={{0,16},{16,0},{1,17},{17,1},{2,18},{18,2},{3,19},{19,3},{4,20},{20... | collective-permute-start | bytes 884744 | tf_op jit(solution)/shard_map/ppermute | solution.py:139
  263.5 26.7 %collective-permute-start.57 = (bf16[1,240,384]{2,1,0:T(8,128)(2,1)S(1)}, bf16[1,240,384]{2,1,0:T(8,128)(2,1)S(1)}, u32[]{:S(2)}, u32[]{:S(2)}) collective-permute-start(bf16[1,240,384]{2,1,0:T(8,128)(2,1)S(1)} %get-tuple-element.141), channel_id=1, source_target_pairs={{0,8},{1,9},{2,10},{3,11},{4,12},{5,13},{6,14},{7,15},{8,0},{9,1},... | collective-permute-start | bytes 552968 | tf_op jit(solution)/shard_map/ppermute | solution.py:139
  263.6 26.6 %collective-permute-start.58 = (f32[272,128]{1,0:T(8,128)S(1)}, f32[272,128]{1,0:T(8,128)S(1)}, u32[]{:S(2)}, u32[]{:S(2)}) collective-permute-start(f32[272,128]{1,0:T(8,128)S(1)} %get-tuple-element.140.refs_2_), channel_id=1, source_target_pairs={{0,8},{1,9},{2,10},{3,11},{4,12},{5,13},{6,14},{7,15},{8,0},{9,1},... | collective-permute-start | bytes 417800 | tf_op jit(solution)/shard_map/ppermute | solution.py:139
  (103 other events, 1146.6 us)
where the time goes:
time: 311 us; the launch traced here: 308 us
  starting transfers between devices  122 us (39%)
  Pallas kernels  110 us (35%)
  waiting for transfers between devices  55.1 us (18%)
  local copies, waits for them, and re-layouts  17.1 us (5%)
    ppermute x23, starting transfers between devices, flip_mask(): return lax.ppermute(block, axis, [(i, i ^ mask) for i in devices])  74.7 us
    pallas_call x5, Pallas kernels, run(): results = inner(span, *after, *carry, *operands)  62.5 us
    pallas_call x13, Pallas kernels, once(): pl.pallas_call(body, grid=(1,), in_specs=[pl.BlockSpec(memory_space=space...  47.2 us
    ppermute x23, waiting for transfers between devices, flip_mask(): return lax.ppermute(block, axis, [(i, i ^ mask) for i in devices])  32.1 us
    ppermute x2, starting transfers between devices, __init__(): self.far = lax.ppermute(block, MESH, far)  20.1 us
    ppermute x9, waiting for transfers between devices, flip_bit(): return lax.ppermute(block, axis, [(i, i ^ 1 << bit) for i in devices])  17.4 us
    unnamed x129, local copies, waits for them, and re-layouts  13.1 us
    ppermute x9, starting transfers between devices, flip_bit(): return lax.ppermute(block, axis, [(i, i ^ 1 << bit) for i in devices])  11 us
  transfers between devices with their start and end apart: 63, of which 12 were waited for; matrix products, arithmetic and copies ran while one was open for 1% of the time, Pallas kernels for 29%

commit v1 on v0

--- a/solution.py
+++ b/solution.py
@@ -142,7 +142,7 @@
 class Sum:
     def __init__(self, kept, sent, stages, left=()):
         self.kept, self.sent, self.stages, self.left = kept, list(sent), list(stages), list(left)
-        self.total = None
+        self.total, self.cut = None, 0
 
     def came(self):
         axis, bit, count = self.stages[0][:3]
@@ -152,7 +152,7 @@
     def plan(self):
         stage = self.stages.pop(0)
         if len(stage) == 4:
-            return ("join",)
+            return ("join", self.cut)
         if self.stages and self.stages[0][0] == "ka" and self.left:
             bit, count = self.stages[0][1] - 1, self.stages[0][2]
             self.left = [b for b in self.left if not bit <= b < bit + count]
@@ -198,10 +198,12 @@
         if plan[0] == "whole":
             out[...] = total(Ellipsis).astype(out.dtype)
         elif plan[0] == "join":
-            half = kept.shape[-1]
+            half, cut = kept.shape[-1], plan[1]
             side = jnp.right_shift(flat, side_bit) & 1
-            out[:, pl.ds(pl.multiple_of(side * half, LANES), half)] = kept[...].astype(F32)
-            out[:, pl.ds(pl.multiple_of((1 - side) * half, LANES), half)] = came[0][...].astype(F32)
+            for ref, rows in ((out, slice(0, cut)), (refs.pop(0), slice(cut, None))):
+                for which, given in ((side, kept), (1 - side, came[0])):
+                    spot = pl.ds(pl.multiple_of(which * half, LANES), half)
+                    ref[:, spot] = given[rows, :].astype(F32)
         else:
             _, bit, count, above, below = plan
             mine = jnp.right_shift(flat, bit + 1) & (2**count - 1)
@@ -223,14 +225,15 @@
         plan = one.plan()
         shape, dtype, size = one.kept.shape, one.kept.dtype, 1
         if plan[0] == "join":
-            shape, dtype = (shape[0], 2 * shape[1]), F32
+            shapes.append(shape_of((plan[1], 2 * shape[1]), F32))
+            shape, dtype = (shape[0] - plan[1], 2 * shape[1]), F32
         elif plan[0] == "part":
             shape, size = (plan[3] * plan[4], *shape[1:]), 2 ** plan[2]
         elif not one.stages:
             dtype = F32
         shapes += [shape_of(shape, dtype)] * size
         plans.append(plan)
-        sizes.append(size)
+        sizes.append(2 if plan[0] == "join" else size)
     results = once(
         functools.partial(stage_kernel, plans, [len(x) for x in came], bits_of("ka")),
         (flat_array, *(one.kept for one in sums), *(x for group in came for x in group)),
@@ -243,7 +246,10 @@
         room=24,
     )
     results = list(results)
-    for one, size in zip(sums, sizes):
+    for one, size, plan in zip(sums, sizes, plans):
+        if plan[0] == "join":
+            one.total = [results.pop(0) for _ in range(size)]
+            continue
         one.kept = results.pop(0)
         one.sent = [results.pop(0) for _ in range(size - 1)] or [one.kept]
         if not one.stages:
@@ -529,7 +535,6 @@
     flat = flat_ref[0]
     chips = len(SLOTS[0]) // 2
     first_block = flat // 2 * 2 - 2 * chips
-    ids = lax.broadcasted_iota(jnp.int32, (LANES, LANES), 0).astype(F32)
     lane = lax.broadcasted_iota(jnp.int32, (1, LANES), 1)
     tables = []
     for k in range(table_ref.shape[0] // 2):
@@ -543,31 +548,37 @@
         ).astype(BF)
         for k in range(length_ref.shape[0])
     ]
+    gathered = [[] for _ in range(7)]
     for b in range(other_ref.shape[1] // LANES):
         block = first_block + b
         inside = (block >= 0) & (block < atoms_blocks)
         source = jnp.clip(block, 0, atoms_blocks - 1)
         at = pl.ds(pl.multiple_of(source * LANES, LANES), LANES)
-        item = jnp.where(inside, item_ref[pl.ds(source, 1), :].astype(F32), -1.0)
-        kind = type_ref[pl.ds(source, 1), :].astype(F32)
-        for k, flag in enumerate(flags):
-            onehot = jnp.where(ids + float(k * LANES) == item, 1.0, 0.0).astype(BF)
-            kind = kind + dot_nn(flag, onehot)[0:1, :]
-        found = jnp.zeros((8, LANES), F32)
-        for k, table in enumerate(tables):
-            onehot = jnp.where(ids + float(k * LANES) == kind, 1.0, 0.0).astype(BF)
-            found = found + dot_nn(table, onehot)
-        rows = [pos_ref[k : k + 1, at] for k in range(3)]
-        rows += [found[0:1] + found[1:2] + found[2:3], found[3:4] + found[4:5] + found[5:6]]
-        rows += [item, open_ref[pl.ds(source, 1), :].astype(F32)]
-        rows += [(block * LANES + lane).astype(F32), kind]
-        rows += [jnp.zeros((SIDE - 9, LANES), F32)]
-        side = jnp.concatenate(rows, axis=0)
-        other_ref[:, b * LANES : (b + 1) * LANES] = side
-
-        @pl.when(block == flat)
-        def _():
-            line_ref[...] = side
+        for k in range(3):
+            gathered[k].append(pos_ref[k : k + 1, at])
+        gathered[3].append(jnp.where(inside, item_ref[pl.ds(source, 1), :].astype(F32), -1.0))
+        gathered[4].append(open_ref[pl.ds(source, 1), :].astype(F32))
+        gathered[5].append((block * LANES + lane).astype(F32))
+        gathered[6].append(type_ref[pl.ds(source, 1), :].astype(F32))
+    rows = [jnp.concatenate(row, axis=1) for row in gathered]
+    item, kind = rows[3], rows[6]
+    ids = lax.broadcasted_iota(jnp.int32, (LANES, item.shape[1]), 0).astype(F32)
+    protein = jnp.zeros_like(kind)
+    for k, flag in enumerate(flags):
+        onehot = jnp.where(ids + float(k * LANES) == item, 1.0, 0.0).astype(BF)
+        protein = protein + dot_nn(flag, onehot)[0:1, :]
+    kind = kind + protein
+    found = jnp.zeros((8, item.shape[1]), F32)
+    for k, table in enumerate(tables):
+        onehot = jnp.where(ids + float(k * LANES) == kind, 1.0, 0.0).astype(BF)
+        found = found + dot_nn(table, onehot)
+    scale = found[0:1] + found[1:2] + found[2:3]
+    shift = found[3:4] + found[4:5] + found[5:6]
+    rows = [*rows[:3], scale, shift, item, rows[4], rows[5], kind]
+    rows.append(jnp.zeros((SIDE - len(rows), item.shape[1]), F32))
+    other_ref[...] = jnp.concatenate(rows, axis=0)
+    own_at = pl.ds(pl.multiple_of((flat - first_block) * LANES, LANES), LANES)
+    line_ref[...] = other_ref[:, own_at]
 
     line = line_ref[...]
     turned = jnp.transpose(
@@ -950,7 +961,7 @@
         wide = jnp.concatenate([by_weight, jnp.zeros((LANES, LANES - heads), F32)], axis=1)
         for k, column in enumerate(columns):
             wide = wide + jnp.where(lane == heads + k, column, 0.0)
-        small_ref[...] = wide
+        small_ref[...] = jnp.transpose(wide)[: small_ref.shape[0]]
 
 
 def middle_kernel(
@@ -1165,6 +1176,7 @@
 def results_kernel(
     heads,
     types,
+    small_rows,
     flat_ref,
     joined_ref,
     first_ref,
@@ -1176,9 +1188,8 @@
     shift_ref,
     pos_ref,
 ):
-    small = joined_ref[:LANES, :]
-    weight_ref[...] = small[:, :heads]
-    turned = jnp.transpose(small)
+    turned = joined_ref[:small_rows, :]
+    weight_ref[...] = turned[:heads]
     rows = [turned[heads + k : heads + k + 1, :] for k in range(6)]
     mean_ref[...] = rows[0]
     width_ref[...] = rows[1]
@@ -1187,8 +1198,8 @@
     count = norm_ref.shape[1]
     for k in range(2):
         norm_ref[k] = first_ref[k * count : (k + 1) * count, :]
-        norm_ref[2 + k] = joined_ref[LANES + k * count : LANES + (k + 1) * count, :]
-    first = LANES + 2 * count
+        norm_ref[2 + k] = joined_ref[small_rows + k * count : small_rows + (k + 1) * count, :]
+    first = small_rows + 2 * count
     blocks = (joined_ref.shape[0] - first) // 3
     for k in range(3):
         spot = first + k * blocks + len(SLOTS[0]) // 2 * 2 + flat_ref[0]
@@ -1670,6 +1681,7 @@
     )
     up_sum = slices_sum(up_kept, up_sent, up_order)
     rest_sum = columns_sum(rest_kept, rest_sent, rest_order)
+    rest_sum.cut = up_rows
 
     dq, grad_scores, window.one, window.two = call(
         functools.partial(query_grad_kernel, scale2, head_scale, groups),
@@ -1696,6 +1708,7 @@
     )(span, own, other, q_aug, do_aug, kvq, bias, select)
 
     pos_blocks = atoms_blocks + 4 * chips
+    small_rows = -(-(heads + 6) // 8) * 8
     small, pos_part = call(
         functools.partial(phi_grad_kernel, 0),
         pairs,
@@ -1708,8 +1721,8 @@
             fixed((kernels, WEIGHT_PIECES * heads)),
             fixed((LANES, LANES)),
         ],
-        [fixed((LANES, LANES)), fixed((3 * pos_blocks, LANES))],
-        [shape_of((LANES, LANES)), shape_of((3 * pos_blocks, LANES))],
+        [fixed((small_rows, LANES)), fixed((3 * pos_blocks, LANES))],
+        [shape_of((small_rows, LANES)), shape_of((3 * pos_blocks, LANES))],
         [
             pltpu.VMEM((own_rows, keys), F32),
             pltpu.VMEM((own_rows, keys), F32),
@@ -1780,7 +1793,6 @@
         "first_norm",
         {0: pltpu.SMEM},
         after=tuple(early_sum.sent),
-        room=24,
     )
     core_stay, core_go = core_flip(to_core), core_flip(to_both)
     chip_own, chip_core = flip_bit(to_chip, "ka", 1), flip_bit(core_go, "ka", 1)
@@ -1814,11 +1826,11 @@
     joined = early_sum.total
     up_total, rest_total = up_sum.total, rest_sum.total
     norms, by_weight, by_mean, by_width, by_scale, by_shift, grad_positions = once(
-        functools.partial(results_kernel, heads, types),
+        functools.partial(results_kernel, heads, types, small_rows),
         (flat_array, joined, norm_sum.total),
         [
             shape_of((4, norm_count, LANES)),
-            shape_of((kernels, heads)),
+            shape_of((heads, kernels)),
             shape_of((1, kernels)),
             shape_of((1, kernels)),
             shape_of((1, types)),
@@ -1841,14 +1853,14 @@
         qkv_total.T,
         by_mean.reshape(-1),
         by_width.reshape(-1),
-        by_weight,
+        by_weight.T,
         by_scale.reshape(-1),
         by_shift.reshape(-1),
-        rest_total[up_rows:].T,
+        rest_total[1].T,
         norms[2].reshape(-1),
         norms[3].reshape(-1),
         up_total.T,
-        rest_total[:up_rows],
+        rest_total[0],
     )
 
 

time: 311 us -> 299 us (0.961)
  starting transfers between devices: 122 us -> 111 us
  waiting for transfers between devices: 55.1 us -> 63.7 us
  local copies, waits for them, and re-layouts: 17.1 us -> 13.6 us
    ppermute x23, starting transfers between devices: 74.7 us -> 55 us  [flip_mask(): return lax.ppermute(block, axis, [(i, i ^ mask) for i in devices])]
    ppermute x2, starting transfers between devices: 20.1 us -> 1.08 us  [__init__(): self.far = lax.ppermute(block, MESH, far)]
    ppermute x25, starting transfers between devices: 6.66 us -> 23.6 us  [core_flip(): return lax.ppermute(block, MESH, [(i, i ^ 1) for i in devices])]
    ppermute x9, starting transfers between devices: 11 us -> 24.4 us  [flip_bit(): return lax.ppermute(block, axis, [(i, i ^ 1 << bit) for i in devices])]
    ppermute x2, waiting for transfers between devices: 1.92 us -> 9.03 us  [__init__(): self.far = lax.ppermute(block, MESH, far)]
    ppermute x2, starting transfers between devices: 6.9 us -> 3.4 us  [__init__(): self.two = lax.ppermute(block, MESH, two)]
    unnamed x129 -> x124, local copies, waits for them, and re-layouts: 13.1 us -> 11.1 us
  transfers between devices with their start and end apart: 63 -> 63, of which waited for: 12 -> 14; matrix products, arithmetic and copies ran while one was open for 1% -> 1% of each run, Pallas kernels for 29% -> 29%
where the time goes in v1:
time: 299 us
  starting transfers between devices  111 us (37%)
  Pallas kernels  107 us (36%)
  waiting for transfers between devices  63.7 us (21%)
  local copies, waits for them, and re-layouts  13.6 us (5%)
    pallas_call x5, Pallas kernels, run(): results = inner(span, *after, *carry, *operands)  61.4 us
    ppermute x23, starting transfers between devices, flip_mask(): return lax.ppermute(block, axis, [(i, i ^ mask) for i in devices])  55 us
    pallas_call x13, Pallas kernels, once(): pl.pallas_call(body, grid=(1,), in_specs=[pl.BlockSpec(memory_space=space...  45.3 us
    ppermute x23, waiting for transfers between devices, flip_mask(): return lax.ppermute(block, axis, [(i, i ^ mask) for i in devices])  34.9 us
    ppermute x9, starting transfers between devices, flip_bit(): return lax.ppermute(block, axis, [(i, i ^ 1 << bit) for i in devices])  24.4 us
    ppermute x25, starting transfers between devices, core_flip(): return lax.ppermute(block, MESH, [(i, i ^ 1) for i in devices])  23.6 us
    ppermute x9, waiting for transfers between devices, flip_bit(): return lax.ppermute(block, axis, [(i, i ^ 1 << bit) for i in devices])  14.9 us
    unnamed x124, local copies, waits for them, and re-layouts  11.1 us
  transfers between devices with their start and end apart: 63, of which 14 were waited for; matrix products, arithmetic and copies ran while one was open for 1% of the time, Pallas kernels for 29%

profile of v1, /device:TPU:0, one launch (start us, length us, event | category | flops | bytes accessed | tf_op | source)
XLA Modules:
  0.0 298.7 jit_solution(3341555432232778942)
XLA Ops:
  19.0 7.1 %collective-permute-done.4.refs_7_ = bf16[128,768]{1,0:T(8,128)(2,1)S(1)} collective-permute-done((bf16[128,768]{1,0:T(8,128)(2,1)}, bf16[128,768]{1,0:T(8,128)(2,1)S(1)}, u32[]{:S(2)}, u32[]{:S(2)}) %collective-permute-start.4) | collective-permute-done | bytes 196640 | tf_op jit(solution)/shard_map/ppermute | solution.py:130
  33.2 7.9 %pair_bias.1.refs_23_.refs_10_.refs_26_ = f32[7,128,32,256]{3,2,1,0:T(8,128)} custom-call(s32[48,128]{1,0:T(8,128)} %get-tuple-element.87.span_ref, bf16[128,768]{1,0:T(8,128)(2,1)} %copy-done.43, bf16[128,768]{1,0:T(8,128)(2,1)} %copy-done.44, bf16[128,768]{1,0:T(8,128)(2,1)} %copy-done.2, f32[128,128]{1,0:T(8,128)} %get-tuple-element.88.refs_3_.refs_1_.refs_5_.refs_0_, ...), custom_call_target="tpu_custom_call" | custom-call | flops 30000001024 | bytes 20000000 | tf_op jit(solution)/shard_map/pair_bias/pallas_call | solution.py:1389
  41.2 11.9 %collective-permute-start.14 = (bf16[2,128,768]{2,1,0:T(8,128)(2,1)S(1)}, bf16[2,128,768]{2,1,0:T(8,128)(2,1)S(1)}, u32[]{:S(2)}, u32[]{:S(2)}) collective-permute-start(bf16[2,128,768]{2,1,0:T(8,128)(2,1)S(1)} %pad_maximum_fusion), channel_id=1, source_target_pairs={{0,4},{1,5},{2,6},{3,7},{4,0},{5,1},{6,2},{7,3},{8,12},{9,13},{10,... | collective-permute-start | bytes 1179656 | tf_op jit(solution)/shard_map/ppermute | solution.py:139
  57.0 17.1 %attention_forward.1 = (f32[128,1024]{1,0:T(8,128)}, bf16[128,1024]{1,0:T(8,128)(2,1)}, bf16[3,128,128]{2,1,0:T(8,128)(2,1)}, bf16[7,256,3072]{2,1,0:T(8,128)(2,1)}) custom-call(s32[48,128]{1,0:T(8,128)} %get-tuple-element.87.span_ref, bf16[128,768]{1,0:T(8,128)(2,1)} %copy-done.20, f32[128,128]{1,0:T(8,128)} %get-tuple-element.88.refs_3_.refs_1_.refs_5_.refs_0_, ...), custom_call_target="tpu_custom_call" | custom-call | flops 24999999488 | bytes 20000000 | tf_op jit(solution)/shard_map/attention_forward/pallas_call | solution.py:1389
  74.1 8.3 %collective-permute-done.15.refs_15_.refs_9_ = bf16[2,128,768]{2,1,0:T(8,128)(2,1)S(1)} collective-permute-done((bf16[2,128,768]{2,1,0:T(8,128)(2,1)S(1)}, bf16[2,128,768]{2,1,0:T(8,128)(2,1)S(1)}, u32[]{:S(2)}, u32[]{:S(2)}) %collective-permute-start.15) | collective-permute-done | bytes 393248 | tf_op jit(solution)/shard_map/ppermute | solution.py:139
  83.3 19.3 %feed_forward.1 = (bf16[128,768]{1,0:T(8,128)(2,1)}, f32[128,768]{1,0:T(8,128)}, bf16[128,1024]{1,0:T(8,128)(2,1)}, bf16[128,1024]{1,0:T(8,128)(2,1)}, bf16[128,...) custom-call(s32[1]{0:T(128)} %bitcast.refs_0_, ...), custom_call_target="tpu_custom_call" | custom-call | flops 10000000000 | bytes 5000000 | tf_op jit(solution)/shard_map/feed_forward/pallas_call | solution.py:1414
  102.6 8.8 %collective-permute-start.17 = (bf16[2,8,192,128]{3,2,1,0:T(8,128)(2,1)}, bf16[2,8,192,128]{3,2,1,0:T(8,128)(2,1)S(1)}, u32[]{:S(2)}, u32[]{:S(2)}) collective-permute-start(bf16[2,8,192,128]{3,2,1,0:T(8,128)(2,1)} %get-tuple-element.96), channel_id=1, source_target_pairs={{0,1},{1,0},{2,3},{3,2},{4,5},{5,4},{6,7},{7,6},{8,9},{9,8},{10,11... | collective-permute-start | bytes 2359304 | tf_op jit(solution)/shard_map/ppermute | solution.py:47
  115.4 4.9 %collective-permute-start.29 = (bf16[128,1024]{1,0:T(8,128)(2,1)}, bf16[128,1024]{1,0:T(8,128)(2,1)}, u32[]{:S(2)}, u32[]{:S(2)}) collective-permute-start(bf16[128,1024]{1,0:T(8,128)(2,1)} %get-tuple-element.99.refs_9_.refs_12_), channel_id=1, source_target_pairs={{0,2},{1,3},{2,0},{3,1},{4,6},{5,7},{6,4},{7,5},{8,10},{9,11},{10,... | collective-permute-start | bytes 786440 | tf_op jit(solution)/shard_map/ppermute | solution.py:130
  120.3 9.0 %collective-permute-done.22.refs_2_.refs_9_ = bf16[128,1024]{1,0:T(8,128)(2,1)S(1)} collective-permute-done((bf16[128,1024]{1,0:T(8,128)(2,1)}, bf16[128,1024]{1,0:T(8,128)(2,1)S(1)}, u32[]{:S(2)}, u32[]{:S(2)}) %collective-permute-start.22) | collective-permute-done | bytes 262176 | tf_op jit(solution)/shard_map/ppermute | solution.py:68
  130.3 9.9 %weight_gradients.1 = (bf16[4,192,768]{2,1,0:T(8,128)(2,1)}, bf16[4,192,768]{2,1,0:T(8,128)(2,1)}, bf16[8,240,384]{2,1,0:T(8,128)(2,1)}, bf16[8,240,384]{2,1,0:T(8,128)(2,1)}) custom-call(s32[1]{0:T(128)} %bitcast.refs_0_, bf16[2,8,192,128]{3,2,1,0:T(8,128)(2,1)} %get-tuple-element.95.refs_1_, bf16[2,8,192,128]{3,2,1,0:T(8,128)(2,1)} %copy-done.22, ...), custom_call_target="tpu_custom_call" | custom-call | flops 5000000000 | bytes 5000000 | tf_op jit(solution)/shard_map/weight_gradients/pallas_call | solution.py:1414
  140.9 11.6 %query_gradients.1 = (bf16[768,128]{1,0:T(8,128)(2,1)}, bf16[7,128,32,256]{3,2,1,0:T(8,128)(2,1)}, bf16[128,1024]{1,0:T(8,128)(2,1)}, bf16[128,1024]{1,0:T(8,128)(2,1)}) custom-call(s32[48,128]{1,0:T(8,128)} %get-tuple-element.87.span_ref, bf16[4,192,768]{2,1,0:T(8,128)(2,1)} %get-tuple-element.100.refs_0_, ...), custom_call_target="tpu_custom_call", output_to_operand_aliasing={{2}: (4, {}), {3}: (5, {})} | custom-call | flops 22000001024 | bytes 20000000 | tf_op jit(solution)/shard_map/query_gradients/pallas_call | solution.py:1389
  152.4 10.5 %collective-permute-start.28 = (bf16[128,1024]{1,0:T(8,128)(2,1)}, bf16[128,1024]{1,0:T(8,128)(2,1)}, u32[]{:S(2)}, u32[]{:S(2)}) collective-permute-start(bf16[128,1024]{1,0:T(8,128)(2,1)} %get-tuple-element.120.refs_10_), channel_id=1, source_target_pairs={{0,2},{1,3},{2,0},{3,1},{4,6},{5,7},{6,4},{7,5},{8,10},{9,11},{10,... | collective-permute-start | bytes 786440 | tf_op jit(solution)/shard_map/ppermute | solution.py:130
  163.0 9.5 %kernel_gradients.1 = (f32[40,128]{1,0:T(8,128)}, f32[132,128]{1,0:T(8,128)}) custom-call(s32[48,128]{1,0:T(8,128)} %get-tuple-element.87.span_ref, f32[128,128]{1,0:T(8,128)} %get-tuple-element.88.refs_3_.refs_1_.refs_5_.refs_0_, f32[16,1792]{1,0:T(8,128)} %get-tuple-element.89.refs_4_.refs_2_.refs_6_.refs_1_, f32[16,128]{1,0:T(8,128)} %get-tuple-element.108.refs_2_, ...), custom_call_target="tpu_custom_call" | custom-call | flops 40000000000 | bytes 20000000 | tf_op jit(solution)/shard_map/kernel_gradients/pallas_call | solution.py:1389
  173.5 23.9 %collective-permute-start.27 = (f32[184,128]{1,0:T(8,128)S(1)}, f32[184,128]{1,0:T(8,128)S(1)}, u32[]{:S(2)}, u32[]{:S(2)}) collective-permute-start(f32[184,128]{1,0:T(8,128)S(1)} %pad_maximum_fusion.1.refs_3_), channel_id=1, source_target_pairs={{0,1},{1,0},{2,3},{3,2},{4,5},{5,4},{6,7},{7,6},{8,9},{9,8},{10,11... | collective-permute-start | bytes 282632 | tf_op jit(solution)/shard_map/ppermute | solution.py:139
  202.5 4.3 %collective-permute-start.39 = (bf16[1,192,768]{2,1,0:T(8,128)(2,1)S(1)}, bf16[1,192,768]{2,1,0:T(8,128)(2,1)S(1)}, u32[]{:S(2)}, u32[]{:S(2)}) collective-permute-start(bf16[1,192,768]{2,1,0:T(8,128)(2,1)S(1)} %get-tuple-element.117.refs_2_), channel_id=1, source_target_pairs={{0,12},{1,13},{2,14},{3,15},{4,8},{5,9},{6,10},{7,11},{8,4},{9,5},... | collective-permute-start | bytes 884744 | tf_op jit(solution)/shard_map/ppermute | solution.py:139
  208.4 15.3 %key_gradients.1.refs_9_.refs_4_ = bf16[1536,128]{1,0:T(8,128)(2,1)} custom-call(s32[48,128]{1,0:T(8,128)} %get-tuple-element.87.span_ref, bf16[1,192,768]{2,1,0:T(8,128)(2,1)} %copy-done.11, bf16[1,192,768]{2,1,0:T(8,128)(2,1)} %copy-done.10, bf16[1,192,768]{2,1,0:T(8,128)(2,1)} %copy-done.9, bf16[4,240,384]{2,1,0:T(8,128)(2,1)} %copy-done.8, ...), custom_call_target="tpu_custom_call" | custom-call | flops 28000000000 | bytes 20000000 | tf_op jit(solution)/shard_map/key_gradients/pallas_call | solution.py:1389
  223.7 10.3 %collective-permute-start.49 = (bf16[128,768]{1,0:T(8,128)(2,1)S(1)}, bf16[128,768]{1,0:T(8,128)(2,1)S(1)}, u32[]{:S(2)}, u32[]{:S(2)}) collective-permute-start(bf16[128,768]{1,0:T(8,128)(2,1)S(1)} %copy-done.3), channel_id=1, source_target_pairs={{0,1},{1,0},{2,3},{3,2},{4,5},{5,4},{6,7},{7,6},{8,9},{9,8},{10,11... | collective-permute-start | bytes 589832 | tf_op jit(solution)/shard_map/ppermute | solution.py:47
  237.4 5.3 %first_norm.1 = (f32[128,768]{1,0:T(8,128)}, bf16[4,160,128]{2,1,0:T(8,128)(2,1)}, bf16[4,160,128]{2,1,0:T(8,128)(2,1)}, bf16[4,160,128]{2,1,0:T(8,128)(2,1)}, bf16[4,160,128]{2,1,0:T(8,128)(2,1)}) custom-call(s32[1]{0:T(128)} %bitcast.refs_0_, bf16[128,768]{1,0:T(8,128)(2,1)} %refs_1_.5, f32[6,128]{1,0:T(8,128)} %bitcast.47, ...), custom_call_target="tpu_custom_call" | custom-call | flops 2000000000 | bytes 5000000 | tf_op jit(solution)/shard_map/first_norm/pallas_call | solution.py:1414
  246.9 4.0 %collective-permute-done.43.refs_2_ = bf16[4,160,128]{2,1,0:T(8,128)(2,1)S(1)} collective-permute-done((bf16[4,160,128]{2,1,0:T(8,128)(2,1)}, bf16[4,160,128]{2,1,0:T(8,128)(2,1)S(1)}, u32[]{:S(2)}, u32[]{:S(2)}) %collective-permute-start.43) | collective-permute-done | bytes 163872 | tf_op jit(solution)/shard_map/ppermute | solution.py:130
  255.2 3.6 %collective-permute-done.56.refs_6_ = f32[184,128]{1,0:T(8,128)S(1)} collective-permute-done((f32[184,128]{1,0:T(8,128)S(1)}, f32[184,128]{1,0:T(8,128)S(1)}, u32[]{:S(2)}, u32[]{:S(2)}) %collective-permute-start.56) | collective-permute-done | bytes 94240 | tf_op jit(solution)/shard_map/ppermute | solution.py:139
  258.9 4.2 %collective-permute-start.48 = (bf16[4,160,128]{2,1,0:T(8,128)(2,1)S(1)}, bf16[4,160,128]{2,1,0:T(8,128)(2,1)S(1)}, u32[]{:S(2)}, u32[]{:S(2)}) collective-permute-start(bf16[4,160,128]{2,1,0:T(8,128)(2,1)S(1)} %get-tuple-element.134), channel_id=1, source_target_pairs={{0,12},{1,13},{2,14},{3,15},{4,8},{5,9},{6,10},{7,11},{8,4},{9,5},... | collective-permute-start | bytes 491528 | tf_op jit(solution)/shard_map/ppermute | solution.py:139
  267.1 11.7 %collective-permute-done.47.refs_2_ = bf16[4,160,128]{2,1,0:T(8,128)(2,1)S(1)} collective-permute-done((bf16[4,160,128]{2,1,0:T(8,128)(2,1)S(1)}, bf16[4,160,128]{2,1,0:T(8,128)(2,1)S(1)}, u32[]{:S(2)}, u32[]{:S(2)}) %collective-permute-start.47) | collective-permute-done | bytes 163872 | tf_op jit(solution)/shard_map/ppermute | solution.py:139
  283.0 4.4 %collective-permute-done.58.refs_4_ = f32[184,128]{1,0:T(8,128)S(1)} collective-permute-done((f32[184,128]{1,0:T(8,128)S(1)}, f32[184,128]{1,0:T(8,128)S(1)}, u32[]{:S(2)}, u32[]{:S(2)}) %collective-permute-start.58) | collective-permute-done | bytes 94240 | tf_op jit(solution)/shard_map/ppermute | solution.py:139
  290.6 5.9 %collective-permute-done.60.refs_6_ = f32[16,128]{1,0:T(8,128)S(1)} collective-permute-done((f32[16,128]{1,0:T(8,128)S(1)}, f32[16,128]{1,0:T(8,128)S(1)}, u32[]{:S(2)}, u32[]{:S(2)}) %collective-permute-start.60) | collective-permute-done | bytes 8224 | tf_op jit(solution)/shard_map/ppermute | solution.py:139
  (250 shorter events, 68.7 us)
Async XLA Ops:
  31.5 21.6 %collective-permute-start.11 = (bf16[128,768]{1,0:T(8,128)(2,1)S(1)}, bf16[128,768]{1,0:T(8,128)(2,1)S(1)}, u32[]{:S(2)}, u32[]{:S(2)}) collective-permute-start(bf16[128,768]{1,0:T(8,128)(2,1)S(1)} %collective-permute-done.4.refs_7_), channel_id=1, source_target_pairs={{0,1},{1,0},{2,3},{3,2},{4,5},{5,4},{6,7},{7,6},{8,9},{9,8},{10,11... | collective-permute-start | bytes 589832 | tf_op jit(solution)/shard_map/ppermute | solution.py:47
  32.1 21.1 %collective-permute-start.7 = (bf16[128,768]{1,0:T(8,128)(2,1)S(1)}, bf16[128,768]{1,0:T(8,128)(2,1)S(1)}, u32[]{:S(2)}, u32[]{:S(2)}) collective-permute-start(bf16[128,768]{1,0:T(8,128)(2,1)S(1)} %collective-permute-done.1.refs_3_), channel_id=1, source_target_pairs={{0,1},{1,0},{2,3},{3,2},{4,5},{5,4},{6,7},{7,6},{8,9},{9,8},{10,11... | collective-permute-start | bytes 589832 | tf_op jit(solution)/shard_map/ppermute | solution.py:47
  32.7 23.0 %collective-permute-start.13 = (bf16[128,768]{1,0:T(8,128)(2,1)S(1)}, bf16[128,768]{1,0:T(8,128)(2,1)S(1)}, u32[]{:S(2)}, u32[]{:S(2)}) collective-permute-start(bf16[128,768]{1,0:T(8,128)(2,1)S(1)} %collective-permute-done.6.refs_9_), channel_id=1, source_target_pairs={{0,1},{1,0},{2,3},{3,2},{4,5},{5,4},{6,7},{7,6},{8,9},{9,8},{10,11... | collective-permute-start | bytes 589832 | tf_op jit(solution)/shard_map/ppermute | solution.py:47
  32.7 22.9 %collective-permute-start.9 = (bf16[128,768]{1,0:T(8,128)(2,1)S(1)}, bf16[128,768]{1,0:T(8,128)(2,1)S(1)}, u32[]{:S(2)}, u32[]{:S(2)}) collective-permute-start(bf16[128,768]{1,0:T(8,128)(2,1)S(1)} %collective-permute-done.3.refs_5_), channel_id=1, source_target_pairs={{0,1},{1,0},{2,3},{3,2},{4,5},{5,4},{6,7},{7,6},{8,9},{9,8},{10,11... | collective-permute-start | bytes 589832 | tf_op jit(solution)/shard_map/ppermute | solution.py:47
  41.2 32.9 %collective-permute-start.14 = (bf16[2,128,768]{2,1,0:T(8,128)(2,1)S(1)}, bf16[2,128,768]{2,1,0:T(8,128)(2,1)S(1)}, u32[]{:S(2)}, u32[]{:S(2)}) collective-permute-start(bf16[2,128,768]{2,1,0:T(8,128)(2,1)S(1)} %pad_maximum_fusion), channel_id=1, source_target_pairs={{0,4},{1,5},{2,6},{3,7},{4,0},{5,1},{6,2},{7,3},{8,12},{9,13},{10,... | collective-permute-start | bytes 1179656 | tf_op jit(solution)/shard_map/ppermute | solution.py:139
  53.2 29.2 %collective-permute-start.15 = (bf16[2,128,768]{2,1,0:T(8,128)(2,1)S(1)}, bf16[2,128,768]{2,1,0:T(8,128)(2,1)S(1)}, u32[]{:S(2)}, u32[]{:S(2)}) collective-permute-start(bf16[2,128,768]{2,1,0:T(8,128)(2,1)S(1)} %pad_maximum_fusion), channel_id=1, source_target_pairs={{0,8},{1,9},{2,10},{3,11},{4,12},{5,13},{6,14},{7,15},{8,0},{9,1},... | collective-permute-start | bytes 1179656 | tf_op jit(solution)/shard_map/ppermute | solution.py:139
  53.2 29.2 %collective-permute-start.16 = (bf16[2,128,768]{2,1,0:T(8,128)(2,1)S(1)}, bf16[2,128,768]{2,1,0:T(8,128)(2,1)S(1)}, u32[]{:S(2)}, u32[]{:S(2)}) collective-permute-start(bf16[2,128,768]{2,1,0:T(8,128)(2,1)S(1)} %pad_maximum_fusion), channel_id=1, source_target_pairs={{0,12},{1,13},{2,14},{3,15},{4,8},{5,9},{6,10},{7,11},{8,4},{9,5},... | collective-permute-start | bytes 1179656 | tf_op jit(solution)/shard_map/ppermute | solution.py:139
  102.6 26.8 %collective-permute-start.17 = (bf16[2,8,192,128]{3,2,1,0:T(8,128)(2,1)}, bf16[2,8,192,128]{3,2,1,0:T(8,128)(2,1)S(1)}, u32[]{:S(2)}, u32[]{:S(2)}) collective-permute-start(bf16[2,8,192,128]{3,2,1,0:T(8,128)(2,1)} %get-tuple-element.96), channel_id=1, source_target_pairs={{0,1},{1,0},{2,3},{3,2},{4,5},{5,4},{6,7},{7,6},{8,9},{9,8},{10,11... | collective-permute-start | bytes 2359304 | tf_op jit(solution)/shard_map/ppermute | solution.py:47
  114.7 25.5 %collective-permute-start.23 = (bf16[128,1024]{1,0:T(8,128)(2,1)}, bf16[128,1024]{1,0:T(8,128)(2,1)}, u32[]{:S(2)}, u32[]{:S(2)}) collective-permute-start(bf16[128,1024]{1,0:T(8,128)(2,1)} %get-tuple-element.99.refs_9_.refs_12_), channel_id=1, source_target_pairs={{0,4},{1,5},{2,6},{3,7},{4,0},{5,1},{6,2},{7,3},{8,12},{9,13},{10,... | collective-permute-start | bytes 786440 | tf_op jit(solution)/shard_map/ppermute | solution.py:66
  115.4 25.5 %collective-permute-start.24 = (bf16[128,1024]{1,0:T(8,128)(2,1)}, bf16[128,1024]{1,0:T(8,128)(2,1)}, u32[]{:S(2)}, u32[]{:S(2)}) collective-permute-start(bf16[128,1024]{1,0:T(8,128)(2,1)} %get-tuple-element.99.refs_9_.refs_12_), channel_id=1, source_target_pairs={{0,28},{1,29},{2,30},{3,31},{4,8},{5,9},{6,10},{7,11},{8,4},{9,5},... | collective-permute-start | bytes 786440 | tf_op jit(solution)/shard_map/ppermute | solution.py:67
  115.4 47.5 %collective-permute-start.29 = (bf16[128,1024]{1,0:T(8,128)(2,1)}, bf16[128,1024]{1,0:T(8,128)(2,1)}, u32[]{:S(2)}, u32[]{:S(2)}) collective-permute-start(bf16[128,1024]{1,0:T(8,128)(2,1)} %get-tuple-element.99.refs_9_.refs_12_), channel_id=1, source_target_pairs={{0,2},{1,3},{2,0},{3,1},{4,6},{5,7},{6,4},{7,5},{8,10},{9,11},{10,... | collective-permute-start | bytes 786440 | tf_op jit(solution)/shard_map/ppermute | solution.py:130
  129.3 44.1 %collective-permute-start.31 = (bf16[128,1024]{1,0:T(8,128)(2,1)S(1)}, bf16[128,1024]{1,0:T(8,128)(2,1)S(1)}, u32[]{:S(2)}, u32[]{:S(2)}) collective-permute-start(bf16[128,1024]{1,0:T(8,128)(2,1)S(1)} %collective-permute-done.22.refs_2_.refs_9_), channel_id=1, source_target_pairs={{0,1},{1,0},{2,3},{3,2},{4,5},{5,4},{6,7},{7,6},{8,9},{9,8},{10,11... | collective-permute-start | bytes 786440 | tf_op jit(solution)/shard_map/ppermute | solution.py:47
  140.2 59.2 %collective-permute-start.26 = (bf16[8,240,384]{2,1,0:T(8,128)(2,1)}, bf16[8,240,384]{2,1,0:T(8,128)(2,1)S(1)}, u32[]{:S(2)}, u32[]{:S(2)}) collective-permute-start(bf16[8,240,384]{2,1,0:T(8,128)(2,1)} %get-tuple-element.101.refs_1_), channel_id=1, source_target_pairs={{0,16},{16,0},{1,17},{17,1},{2,18},{18,2},{3,19},{19,3},{4,20},{20... | collective-permute-start | bytes 4423688 | tf_op jit(solution)/shard_map/ppermute | solution.py:139
  140.2 59.0 %collective-permute-start.25 = (bf16[4,192,768]{2,1,0:T(8,128)(2,1)}, bf16[4,192,768]{2,1,0:T(8,128)(2,1)S(1)}, u32[]{:S(2)}, u32[]{:S(2)}) collective-permute-start(bf16[4,192,768]{2,1,0:T(8,128)(2,1)} %get-tuple-element.100.refs_0_), channel_id=1, source_target_pairs={{0,2},{1,3},{2,0},{3,1},{4,6},{5,7},{6,4},{7,5},{8,10},{9,11},{10,... | collective-permute-start | bytes 3538952 | tf_op jit(solution)/shard_map/ppermute | solution.py:139
  152.4 46.3 %collective-permute-start.28 = (bf16[128,1024]{1,0:T(8,128)(2,1)}, bf16[128,1024]{1,0:T(8,128)(2,1)}, u32[]{:S(2)}, u32[]{:S(2)}) collective-permute-start(bf16[128,1024]{1,0:T(8,128)(2,1)} %get-tuple-element.120.refs_10_), channel_id=1, source_target_pairs={{0,2},{1,3},{2,0},{3,1},{4,6},{5,7},{6,4},{7,5},{8,10},{9,11},{10,... | collective-permute-start | bytes 786440 | tf_op jit(solution)/shard_map/ppermute | solution.py:130
  162.9 35.9 %collective-permute-start.30 = (bf16[128,1024]{1,0:T(8,128)(2,1)}, bf16[128,1024]{1,0:T(8,128)(2,1)}, u32[]{:S(2)}, u32[]{:S(2)}) collective-permute-start(bf16[128,1024]{1,0:T(8,128)(2,1)} %get-tuple-element.121.refs_14_), channel_id=1, source_target_pairs={{0,2},{1,3},{2,0},{3,1},{4,6},{5,7},{6,4},{7,5},{8,10},{9,11},{10,... | collective-permute-start | bytes 786440 | tf_op jit(solution)/shard_map/ppermute | solution.py:130
  173.5 24.9 %collective-permute-start.27 = (f32[184,128]{1,0:T(8,128)S(1)}, f32[184,128]{1,0:T(8,128)S(1)}, u32[]{:S(2)}, u32[]{:S(2)}) collective-permute-start(f32[184,128]{1,0:T(8,128)S(1)} %pad_maximum_fusion.1.refs_3_), channel_id=1, source_target_pairs={{0,1},{1,0},{2,3},{3,2},{4,5},{5,4},{6,7},{7,6},{8,9},{9,8},{10,11... | collective-permute-start | bytes 282632 | tf_op jit(solution)/shard_map/ppermute | solution.py:139
  201.2 33.4 %collective-permute-start.40 = (bf16[4,240,384]{2,1,0:T(8,128)(2,1)S(1)}, bf16[4,240,384]{2,1,0:T(8,128)(2,1)S(1)}, u32[]{:S(2)}, u32[]{:S(2)}) collective-permute-start(bf16[4,240,384]{2,1,0:T(8,128)(2,1)S(1)} %get-tuple-element.118.refs_3_), channel_id=1, source_target_pairs={{0,2},{1,3},{2,0},{3,1},{4,6},{5,7},{6,4},{7,5},{8,10},{9,11},{10,... | collective-permute-start | bytes 2211848 | tf_op jit(solution)/shard_map/ppermute | solution.py:139
  202.3 31.7 %collective-permute-start.37 = (bf16[1,192,768]{2,1,0:T(8,128)(2,1)S(1)}, bf16[1,192,768]{2,1,0:T(8,128)(2,1)S(1)}, u32[]{:S(2)}, u32[]{:S(2)}) collective-permute-start(bf16[1,192,768]{2,1,0:T(8,128)(2,1)S(1)} %get-tuple-element.115.refs_0_), channel_id=1, source_target_pairs={{0,4},{1,5},{2,6},{3,7},{4,0},{5,1},{6,2},{7,3},{8,12},{9,13},{10,... | collective-permute-start | bytes 884744 | tf_op jit(solution)/shard_map/ppermute | solution.py:139
  202.4 31.8 %collective-permute-start.38 = (bf16[1,192,768]{2,1,0:T(8,128)(2,1)S(1)}, bf16[1,192,768]{2,1,0:T(8,128)(2,1)S(1)}, u32[]{:S(2)}, u32[]{:S(2)}) collective-permute-start(bf16[1,192,768]{2,1,0:T(8,128)(2,1)S(1)} %get-tuple-element.116.refs_1_), channel_id=1, source_target_pairs={{0,8},{1,9},{2,10},{3,11},{4,12},{5,13},{6,14},{7,15},{8,0},{9,1},... | collective-permute-start | bytes 884744 | tf_op jit(solution)/shard_map/ppermute | solution.py:139
  202.5 32.1 %collective-permute-start.39 = (bf16[1,192,768]{2,1,0:T(8,128)(2,1)S(1)}, bf16[1,192,768]{2,1,0:T(8,128)(2,1)S(1)}, u32[]{:S(2)}, u32[]{:S(2)}) collective-permute-start(bf16[1,192,768]{2,1,0:T(8,128)(2,1)S(1)} %get-tuple-element.117.refs_2_), channel_id=1, source_target_pairs={{0,12},{1,13},{2,14},{3,15},{4,8},{5,9},{6,10},{7,11},{8,4},{9,5},... | collective-permute-start | bytes 884744 | tf_op jit(solution)/shard_map/ppermute | solution.py:139
  258.9 19.9 %collective-permute-start.47 = (bf16[4,160,128]{2,1,0:T(8,128)(2,1)S(1)}, bf16[4,160,128]{2,1,0:T(8,128)(2,1)S(1)}, u32[]{:S(2)}, u32[]{:S(2)}) collective-permute-start(bf16[4,160,128]{2,1,0:T(8,128)(2,1)S(1)} %get-tuple-element.133), channel_id=1, source_target_pairs={{0,8},{1,9},{2,10},{3,11},{4,12},{5,13},{6,14},{7,15},{8,0},{9,1},... | collective-permute-start | bytes 491528 | tf_op jit(solution)/shard_map/ppermute | solution.py:139
  264.1 23.3 %collective-permute-start.57 = (bf16[1,240,384]{2,1,0:T(8,128)(2,1)S(1)}, bf16[1,240,384]{2,1,0:T(8,128)(2,1)S(1)}, u32[]{:S(2)}, u32[]{:S(2)}) collective-permute-start(bf16[1,240,384]{2,1,0:T(8,128)(2,1)S(1)} %get-tuple-element.142), channel_id=1, source_target_pairs={{0,8},{1,9},{2,10},{3,11},{4,12},{5,13},{6,14},{7,15},{8,0},{9,1},... | collective-permute-start | bytes 552968 | tf_op jit(solution)/shard_map/ppermute | solution.py:139
  264.2 23.2 %collective-permute-start.58 = (f32[184,128]{1,0:T(8,128)S(1)}, f32[184,128]{1,0:T(8,128)S(1)}, u32[]{:S(2)}, u32[]{:S(2)}) collective-permute-start(f32[184,128]{1,0:T(8,128)S(1)} %get-tuple-element.141.refs_2_), channel_id=1, source_target_pairs={{0,8},{1,9},{2,10},{3,11},{4,12},{5,13},{6,14},{7,15},{8,0},{9,1},... | collective-permute-start | bytes 282632 | tf_op jit(solution)/shard_map/ppermute | solution.py:139
  (101 other events, 1017.9 us)

commit v2 on v1

--- a/solution.py
+++ b/solution.py
@@ -1030,7 +1030,7 @@
     down_ref[...] = mixed
     back_ref[...] = jnp.zeros(back_ref.shape, F32)
 
-    def step(t, carry):
+    def step(t):
         for copy in tile_copies(t):
             copy.wait()
         spot = pl.ds(pl.multiple_of(t * tile, LANES), tile)
@@ -1058,9 +1058,13 @@
 
         down_ref[...] += dot_nn(hidden, wdown_ref[spot, :])
         back_ref[...] += dot_nt(grad_up, wup_ref[:, spot])
+
+    def two_steps(i, carry):
+        step(2 * i)
+        step(2 * i + 1)
         return carry
 
-    lax.fori_loop(0, tiles, step, 0)
+    lax.fori_loop(0, tiles // 2, two_steps, 0)
     out_ref[...] = down_ref[...].astype(BF)
     back, by_gain, by_shift = norm_back(back_ref[...], normal, slope, gain)
     lngrad_ref[...] = jnp.concatenate([by_gain, by_shift], axis=0)
@@ -1113,25 +1117,21 @@
     def columns(which):
         return pl.ds(pl.multiple_of(which * half, LANES), half)
 
-    def step(m, carry):
-        both = jnp.concatenate([mine_ref[0, m], came_ref[0, m]], axis=1)
-        value = dot_nn(both, normed).astype(BF)
-
-        @pl.when(m % 2 == bit)
-        def _():
-            up_kept_ref[m // 2] = value
-
-        @pl.when(m % 2 != bit)
-        def _():
-            up_sent_ref[m // 2] = value
-
-        both = jnp.concatenate([mine_ref[1, m], came_ref[1, m]], axis=1)
-        product_ref[:rows, :] = dot_nn(both, cotangent)
-        rest_kept_ref[m, :rows, :] = product_ref[:rows, columns(side)].astype(BF)
-        rest_sent_ref[m, :rows, :] = product_ref[:rows, columns(1 - side)].astype(BF)
+    def step(pair, carry):
+        for which, ref in ((bit, up_kept_ref), (1 - bit, up_sent_ref)):
+            m = 2 * pair + which
+            both = jnp.concatenate([mine_ref[0, m], came_ref[0, m]], axis=1)
+            ref[pair] = dot_nn(both, normed).astype(BF)
+        for k in range(2):
+            m = 2 * pair + k
+            both = jnp.concatenate([mine_ref[1, m], came_ref[1, m]], axis=1)
+            spot = slice(k * rows, (k + 1) * rows)
+            product_ref[spot, :] = dot_nn(both, cotangent)
+            rest_kept_ref[m, :rows, :] = product_ref[spot, columns(side)].astype(BF)
+            rest_sent_ref[m, :rows, :] = product_ref[spot, columns(1 - side)].astype(BF)
         return carry
 
-    lax.fori_loop(0, slices, step, 0)
+    lax.fori_loop(0, slices // 2, step, 0)
     grads = jnp.concatenate(
         [payload_ref[:, :model_width], payload_came_ref[:, :model_width]], axis=0
     )

time: 299 us -> 298 us (level)
  starting transfers between devices: 111 us -> 121 us
  waiting for transfers between devices: 63.7 us -> 58.1 us
  Pallas kernels: 107 us -> 104 us
    ppermute x25, starting transfers between devices: 23.6 us -> 6.23 us  [core_flip(): return lax.ppermute(block, MESH, [(i, i ^ 1) for i in devices])]
    ppermute x9, starting transfers between devices: 24.4 us -> 38.5 us  [flip_bit(): return lax.ppermute(block, axis, [(i, i ^ 1 << bit) for i in devices])]
    ppermute x2, waiting for transfers between devices: 9.03 us -> 0.01 us  [__init__(): self.far = lax.ppermute(block, MESH, far)]
    ppermute x2, starting transfers between devices: 3.66 us -> 11.9 us  [__init__(): self.one = lax.ppermute(block, MESH, one)]
    ppermute x23, starting transfers between devices: 55 us -> 59.6 us  [flip_mask(): return lax.ppermute(block, axis, [(i, i ^ mask) for i in devices])]
    ppermute x9, waiting for transfers between devices: 14.9 us -> 18.2 us  [flip_bit(): return lax.ppermute(block, axis, [(i, i ^ 1 << bit) for i in devices])]
    pallas_call x13, Pallas kernels: 45.3 us -> 42.1 us  [once(): pl.pallas_call(body, grid=(1,), in_specs=[pl.BlockSpec(memory_space=space...]
  transfers between devices with their start and end apart: 63 -> 63, of which waited for: 14 -> 14; matrix products, arithmetic and copies ran while one was open for 1% -> 1% of each run, Pallas kernels for 29% -> 28%
where the time goes in v2:
time: 298 us; the launch traced here: 300 us
  starting transfers between devices  121 us (41%)
  Pallas kernels  104 us (35%)
  waiting for transfers between devices  58.1 us (19%)
  local copies, waits for them, and re-layouts  13.6 us (5%)
    pallas_call x5, Pallas kernels, run(): results = inner(span, *after, *carry, *operands)  61.5 us
    ppermute x23, starting transfers between devices, flip_mask(): return lax.ppermute(block, axis, [(i, i ^ mask) for i in devices])  59.6 us
    pallas_call x13, Pallas kernels, once(): pl.pallas_call(body, grid=(1,), in_specs=[pl.BlockSpec(memory_space=space...  42.1 us
    ppermute x9, starting transfers between devices, flip_bit(): return lax.ppermute(block, axis, [(i, i ^ 1 << bit) for i in devices])  38.5 us
    ppermute x23, waiting for transfers between devices, flip_mask(): return lax.ppermute(block, axis, [(i, i ^ mask) for i in devices])  35.3 us
    ppermute x9, waiting for transfers between devices, flip_bit(): return lax.ppermute(block, axis, [(i, i ^ 1 << bit) for i in devices])  18.2 us
    ppermute x2, starting transfers between devices, __init__(): self.one = lax.ppermute(block, MESH, one)  11.9 us
    unnamed x124, local copies, waits for them, and re-layouts  11.1 us
  transfers between devices with their start and end apart: 63, of which 14 were waited for; matrix products, arithmetic and copies ran while one was open for 1% of the time, Pallas kernels for 28%

profile of v2, /device:TPU:0, one launch (start us, length us, event | category | flops | bytes accessed | tf_op | source)
XLA Modules:
  0.0 299.7 jit_solution(8832132767423225685)
XLA Ops:
  19.0 7.1 %collective-permute-done.4.refs_7_ = bf16[128,768]{1,0:T(8,128)(2,1)S(1)} collective-permute-done((bf16[128,768]{1,0:T(8,128)(2,1)}, bf16[128,768]{1,0:T(8,128)(2,1)S(1)}, u32[]{:S(2)}, u32[]{:S(2)}) %collective-permute-start.4) | collective-permute-done | bytes 196640 | tf_op jit(solution)/shard_map/ppermute | solution.py:130
  33.2 7.9 %pair_bias.1.refs_23_.refs_10_.refs_26_ = f32[7,128,32,256]{3,2,1,0:T(8,128)} custom-call(s32[48,128]{1,0:T(8,128)} %get-tuple-element.87.span_ref, bf16[128,768]{1,0:T(8,128)(2,1)} %copy-done.43, bf16[128,768]{1,0:T(8,128)(2,1)} %copy-done.44, bf16[128,768]{1,0:T(8,128)(2,1)} %copy-done.2, f32[128,128]{1,0:T(8,128)} %get-tuple-element.88.refs_3_.refs_1_.refs_5_.refs_0_, ...), custom_call_target="tpu_custom_call" | custom-call | flops 30000001024 | bytes 20000000 | tf_op jit(solution)/shard_map/pair_bias/pallas_call | solution.py:1389
  41.2 12.0 %collective-permute-start.14 = (bf16[2,128,768]{2,1,0:T(8,128)(2,1)S(1)}, bf16[2,128,768]{2,1,0:T(8,128)(2,1)S(1)}, u32[]{:S(2)}, u32[]{:S(2)}) collective-permute-start(bf16[2,128,768]{2,1,0:T(8,128)(2,1)S(1)} %pad_maximum_fusion), channel_id=1, source_target_pairs={{0,4},{1,5},{2,6},{3,7},{4,0},{5,1},{6,2},{7,3},{8,12},{9,13},{10,... | collective-permute-start | bytes 1179656 | tf_op jit(solution)/shard_map/ppermute | solution.py:139
  57.0 17.1 %attention_forward.1 = (f32[128,1024]{1,0:T(8,128)}, bf16[128,1024]{1,0:T(8,128)(2,1)}, bf16[3,128,128]{2,1,0:T(8,128)(2,1)}, bf16[7,256,3072]{2,1,0:T(8,128)(2,1)}) custom-call(s32[48,128]{1,0:T(8,128)} %get-tuple-element.87.span_ref, bf16[128,768]{1,0:T(8,128)(2,1)} %copy-done.20, f32[128,128]{1,0:T(8,128)} %get-tuple-element.88.refs_3_.refs_1_.refs_5_.refs_0_, ...), custom_call_target="tpu_custom_call" | custom-call | flops 24999999488 | bytes 20000000 | tf_op jit(solution)/shard_map/attention_forward/pallas_call | solution.py:1389
  74.2 7.5 %collective-permute-done.15.refs_15_.refs_9_ = bf16[2,128,768]{2,1,0:T(8,128)(2,1)S(1)} collective-permute-done((bf16[2,128,768]{2,1,0:T(8,128)(2,1)S(1)}, bf16[2,128,768]{2,1,0:T(8,128)(2,1)S(1)}, u32[]{:S(2)}, u32[]{:S(2)}) %collective-permute-start.15) | collective-permute-done | bytes 393248 | tf_op jit(solution)/shard_map/ppermute | solution.py:139
  82.6 18.6 %feed_forward.1 = (bf16[128,768]{1,0:T(8,128)(2,1)}, f32[128,768]{1,0:T(8,128)}, bf16[128,1024]{1,0:T(8,128)(2,1)}, bf16[128,1024]{1,0:T(8,128)(2,1)}, bf16[128,...) custom-call(s32[1]{0:T(128)} %bitcast.refs_0_, ...), custom_call_target="tpu_custom_call" | custom-call | flops 10000000000 | bytes 5000000 | tf_op jit(solution)/shard_map/feed_forward/pallas_call | solution.py:1414
  104.8 8.9 %collective-permute-start.23 = (bf16[128,1024]{1,0:T(8,128)(2,1)}, bf16[128,1024]{1,0:T(8,128)(2,1)}, u32[]{:S(2)}, u32[]{:S(2)}) collective-permute-start(bf16[128,1024]{1,0:T(8,128)(2,1)} %get-tuple-element.99.refs_9_.refs_12_), channel_id=1, source_target_pairs={{0,4},{1,5},{2,6},{3,7},{4,0},{5,1},{6,2},{7,3},{8,12},{9,13},{10,... | collective-permute-start | bytes 786440 | tf_op jit(solution)/shard_map/ppermute | solution.py:66
  113.7 7.6 %collective-permute-start.29 = (bf16[128,1024]{1,0:T(8,128)(2,1)}, bf16[128,1024]{1,0:T(8,128)(2,1)}, u32[]{:S(2)}, u32[]{:S(2)}) collective-permute-start(bf16[128,1024]{1,0:T(8,128)(2,1)} %get-tuple-element.99.refs_9_.refs_12_), channel_id=1, source_target_pairs={{0,2},{1,3},{2,0},{3,1},{4,6},{5,7},{6,4},{7,5},{8,10},{9,11},{10,... | collective-permute-start | bytes 786440 | tf_op jit(solution)/shard_map/ppermute | solution.py:130
  122.3 7.3 %weight_gradients.1 = (bf16[4,192,768]{2,1,0:T(8,128)(2,1)}, bf16[4,192,768]{2,1,0:T(8,128)(2,1)}, bf16[8,240,384]{2,1,0:T(8,128)(2,1)}, bf16[8,240,384]{2,1,0:T(8,128)(2,1)}) custom-call(s32[1]{0:T(128)} %bitcast.refs_0_, bf16[2,8,192,128]{3,2,1,0:T(8,128)(2,1)} %get-tuple-element.95.refs_1_, bf16[2,8,192,128]{3,2,1,0:T(8,128)(2,1)} %copy-done.22, ...), custom_call_target="tpu_custom_call" | custom-call | flops 5000000000 | bytes 5000000 | tf_op jit(solution)/shard_map/weight_gradients/pallas_call | solution.py:1414
  132.8 4.8 %collective-permute-start.25 = (bf16[4,192,768]{2,1,0:T(8,128)(2,1)}, bf16[4,192,768]{2,1,0:T(8,128)(2,1)S(1)}, u32[]{:S(2)}, u32[]{:S(2)}) collective-permute-start(bf16[4,192,768]{2,1,0:T(8,128)(2,1)} %get-tuple-element.100.refs_0_), channel_id=1, source_target_pairs={{0,2},{1,3},{2,0},{3,1},{4,6},{5,7},{6,4},{7,5},{8,10},{9,11},{10,... | collective-permute-start | bytes 3538952 | tf_op jit(solution)/shard_map/ppermute | solution.py:139
  137.6 11.6 %query_gradients.1 = (bf16[768,128]{1,0:T(8,128)(2,1)}, bf16[7,128,32,256]{3,2,1,0:T(8,128)(2,1)}, bf16[128,1024]{1,0:T(8,128)(2,1)}, bf16[128,1024]{1,0:T(8,128)(2,1)}) custom-call(s32[48,128]{1,0:T(8,128)} %get-tuple-element.87.span_ref, bf16[4,192,768]{2,1,0:T(8,128)(2,1)} %get-tuple-element.100.refs_0_, ...), custom_call_target="tpu_custom_call", output_to_operand_aliasing={{2}: (4, {}), {3}: (5, {})} | custom-call | flops 22000001024 | bytes 20000000 | tf_op jit(solution)/shard_map/query_gradients/pallas_call | solution.py:1389
  149.1 10.8 %collective-permute-start.28 = (bf16[128,1024]{1,0:T(8,128)(2,1)}, bf16[128,1024]{1,0:T(8,128)(2,1)}, u32[]{:S(2)}, u32[]{:S(2)}) collective-permute-start(bf16[128,1024]{1,0:T(8,128)(2,1)} %get-tuple-element.120.refs_10_), channel_id=1, source_target_pairs={{0,2},{1,3},{2,0},{3,1},{4,6},{5,7},{6,4},{7,5},{8,10},{9,11},{10,... | collective-permute-start | bytes 786440 | tf_op jit(solution)/shard_map/ppermute | solution.py:130
  160.0 9.5 %kernel_gradients.1 = (f32[40,128]{1,0:T(8,128)}, f32[132,128]{1,0:T(8,128)}) custom-call(s32[48,128]{1,0:T(8,128)} %get-tuple-element.87.span_ref, f32[128,128]{1,0:T(8,128)} %get-tuple-element.88.refs_3_.refs_1_.refs_5_.refs_0_, f32[16,1792]{1,0:T(8,128)} %get-tuple-element.89.refs_4_.refs_2_.refs_6_.refs_1_, f32[16,128]{1,0:T(8,128)} %get-tuple-element.108.refs_2_, ...), custom_call_target="tpu_custom_call" | custom-call | flops 40000000000 | bytes 20000000 | tf_op jit(solution)/shard_map/kernel_gradients/pallas_call | solution.py:1389
  177.7 23.1 %collective-permute-start.40 = (bf16[4,240,384]{2,1,0:T(8,128)(2,1)S(1)}, bf16[4,240,384]{2,1,0:T(8,128)(2,1)S(1)}, u32[]{:S(2)}, u32[]{:S(2)}) collective-permute-start(bf16[4,240,384]{2,1,0:T(8,128)(2,1)S(1)} %get-tuple-element.118.refs_3_), channel_id=1, source_target_pairs={{0,2},{1,3},{2,0},{3,1},{4,6},{5,7},{6,4},{7,5},{8,10},{9,11},{10,... | collective-permute-start | bytes 2211848 | tf_op jit(solution)/shard_map/ppermute | solution.py:139
  200.9 4.3 %collective-permute-start.39 = (bf16[1,192,768]{2,1,0:T(8,128)(2,1)S(1)}, bf16[1,192,768]{2,1,0:T(8,128)(2,1)S(1)}, u32[]{:S(2)}, u32[]{:S(2)}) collective-permute-start(bf16[1,192,768]{2,1,0:T(8,128)(2,1)S(1)} %get-tuple-element.117.refs_2_), channel_id=1, source_target_pairs={{0,12},{1,13},{2,14},{3,15},{4,8},{5,9},{6,10},{7,11},{8,4},{9,5},... | collective-permute-start | bytes 884744 | tf_op jit(solution)/shard_map/ppermute | solution.py:139
  206.0 15.4 %key_gradients.1.refs_9_.refs_4_ = bf16[1536,128]{1,0:T(8,128)(2,1)} custom-call(s32[48,128]{1,0:T(8,128)} %get-tuple-element.87.span_ref, bf16[1,192,768]{2,1,0:T(8,128)(2,1)} %copy-done.11, bf16[1,192,768]{2,1,0:T(8,128)(2,1)} %copy-done.10, bf16[1,192,768]{2,1,0:T(8,128)(2,1)} %copy-done.9, bf16[4,240,384]{2,1,0:T(8,128)(2,1)} %copy-done.8, ...), custom_call_target="tpu_custom_call" | custom-call | flops 28000000000 | bytes 20000000 | tf_op jit(solution)/shard_map/key_gradients/pallas_call | solution.py:1389
  227.2 5.3 %first_norm.1 = (f32[128,768]{1,0:T(8,128)}, bf16[4,160,128]{2,1,0:T(8,128)(2,1)}, bf16[4,160,128]{2,1,0:T(8,128)(2,1)}, bf16[4,160,128]{2,1,0:T(8,128)(2,1)}, bf16[4,160,128]{2,1,0:T(8,128)(2,1)}) custom-call(s32[1]{0:T(128)} %bitcast.refs_0_, bf16[128,768]{1,0:T(8,128)(2,1)} %refs_1_.5, f32[6,128]{1,0:T(8,128)} %bitcast.47, ...), custom_call_target="tpu_custom_call" | custom-call | flops 2000000000 | bytes 5000000 | tf_op jit(solution)/shard_map/first_norm/pallas_call | solution.py:1414
  233.0 13.6 %collective-permute-start.43 = (bf16[4,160,128]{2,1,0:T(8,128)(2,1)}, bf16[4,160,128]{2,1,0:T(8,128)(2,1)S(1)}, u32[]{:S(2)}, u32[]{:S(2)}) collective-permute-start(bf16[4,160,128]{2,1,0:T(8,128)(2,1)} %get-tuple-element.129), channel_id=1, source_target_pairs={{0,2},{1,3},{2,0},{3,1},{4,6},{5,7},{6,4},{7,5},{8,10},{9,11},{10,... | collective-permute-start | bytes 491528 | tf_op jit(solution)/shard_map/ppermute | solution.py:130
  247.9 4.0 %collective-permute-done.43.refs_2_ = bf16[4,160,128]{2,1,0:T(8,128)(2,1)S(1)} collective-permute-done((bf16[4,160,128]{2,1,0:T(8,128)(2,1)}, bf16[4,160,128]{2,1,0:T(8,128)(2,1)S(1)}, u32[]{:S(2)}, u32[]{:S(2)}) %collective-permute-start.43) | collective-permute-done | bytes 163872 | tf_op jit(solution)/shard_map/ppermute | solution.py:130
  256.1 3.6 %collective-permute-done.56.refs_6_ = f32[184,128]{1,0:T(8,128)S(1)} collective-permute-done((f32[184,128]{1,0:T(8,128)S(1)}, f32[184,128]{1,0:T(8,128)S(1)}, u32[]{:S(2)}, u32[]{:S(2)}) %collective-permute-start.56) | collective-permute-done | bytes 94240 | tf_op jit(solution)/shard_map/ppermute | solution.py:139
  259.9 4.2 %collective-permute-start.48 = (bf16[4,160,128]{2,1,0:T(8,128)(2,1)S(1)}, bf16[4,160,128]{2,1,0:T(8,128)(2,1)S(1)}, u32[]{:S(2)}, u32[]{:S(2)}) collective-permute-start(bf16[4,160,128]{2,1,0:T(8,128)(2,1)S(1)} %get-tuple-element.134), channel_id=1, source_target_pairs={{0,12},{1,13},{2,14},{3,15},{4,8},{5,9},{6,10},{7,11},{8,4},{9,5},... | collective-permute-start | bytes 491528 | tf_op jit(solution)/shard_map/ppermute | solution.py:139
  268.0 11.7 %collective-permute-done.47.refs_2_ = bf16[4,160,128]{2,1,0:T(8,128)(2,1)S(1)} collective-permute-done((bf16[4,160,128]{2,1,0:T(8,128)(2,1)S(1)}, bf16[4,160,128]{2,1,0:T(8,128)(2,1)S(1)}, u32[]{:S(2)}, u32[]{:S(2)}) %collective-permute-start.47) | collective-permute-done | bytes 163872 | tf_op jit(solution)/shard_map/ppermute | solution.py:139
  283.9 4.4 %collective-permute-done.58.refs_4_ = f32[184,128]{1,0:T(8,128)S(1)} collective-permute-done((f32[184,128]{1,0:T(8,128)S(1)}, f32[184,128]{1,0:T(8,128)S(1)}, u32[]{:S(2)}, u32[]{:S(2)}) %collective-permute-start.58) | collective-permute-done | bytes 94240 | tf_op jit(solution)/shard_map/ppermute | solution.py:139
  291.5 5.9 %collective-permute-done.60.refs_6_ = f32[16,128]{1,0:T(8,128)S(1)} collective-permute-done((f32[16,128]{1,0:T(8,128)S(1)}, f32[16,128]{1,0:T(8,128)S(1)}, u32[]{:S(2)}, u32[]{:S(2)}) %collective-permute-start.60) | collective-permute-done | bytes 8224 | tf_op jit(solution)/shard_map/ppermute | solution.py:139
  (250 shorter events, 72.2 us)
Async XLA Ops:
  32.7 23.0 %collective-permute-start.13 = (bf16[128,768]{1,0:T(8,128)(2,1)S(1)}, bf16[128,768]{1,0:T(8,128)(2,1)S(1)}, u32[]{:S(2)}, u32[]{:S(2)}) collective-permute-start(bf16[128,768]{1,0:T(8,128)(2,1)S(1)} %collective-permute-done.6.refs_9_), channel_id=1, source_target_pairs={{0,1},{1,0},{2,3},{3,2},{4,5},{5,4},{6,7},{7,6},{8,9},{9,8},{10,11... | collective-permute-start | bytes 589832 | tf_op jit(solution)/shard_map/ppermute | solution.py:47
  32.7 23.0 %collective-permute-start.9 = (bf16[128,768]{1,0:T(8,128)(2,1)S(1)}, bf16[128,768]{1,0:T(8,128)(2,1)S(1)}, u32[]{:S(2)}, u32[]{:S(2)}) collective-permute-start(bf16[128,768]{1,0:T(8,128)(2,1)S(1)} %collective-permute-done.3.refs_5_), channel_id=1, source_target_pairs={{0,1},{1,0},{2,3},{3,2},{4,5},{5,4},{6,7},{7,6},{8,9},{9,8},{10,11... | collective-permute-start | bytes 589832 | tf_op jit(solution)/shard_map/ppermute | solution.py:47
  41.2 32.9 %collective-permute-start.14 = (bf16[2,128,768]{2,1,0:T(8,128)(2,1)S(1)}, bf16[2,128,768]{2,1,0:T(8,128)(2,1)S(1)}, u32[]{:S(2)}, u32[]{:S(2)}) collective-permute-start(bf16[2,128,768]{2,1,0:T(8,128)(2,1)S(1)} %pad_maximum_fusion), channel_id=1, source_target_pairs={{0,4},{1,5},{2,6},{3,7},{4,0},{5,1},{6,2},{7,3},{8,12},{9,13},{10,... | collective-permute-start | bytes 1179656 | tf_op jit(solution)/shard_map/ppermute | solution.py:139
  53.2 28.5 %collective-permute-start.15 = (bf16[2,128,768]{2,1,0:T(8,128)(2,1)S(1)}, bf16[2,128,768]{2,1,0:T(8,128)(2,1)S(1)}, u32[]{:S(2)}, u32[]{:S(2)}) collective-permute-start(bf16[2,128,768]{2,1,0:T(8,128)(2,1)S(1)} %pad_maximum_fusion), channel_id=1, source_target_pairs={{0,8},{1,9},{2,10},{3,11},{4,12},{5,13},{6,14},{7,15},{8,0},{9,1},... | collective-permute-start | bytes 1179656 | tf_op jit(solution)/shard_map/ppermute | solution.py:139
  53.2 28.4 %collective-permute-start.16 = (bf16[2,128,768]{2,1,0:T(8,128)(2,1)S(1)}, bf16[2,128,768]{2,1,0:T(8,128)(2,1)S(1)}, u32[]{:S(2)}, u32[]{:S(2)}) collective-permute-start(bf16[2,128,768]{2,1,0:T(8,128)(2,1)S(1)} %pad_maximum_fusion), channel_id=1, source_target_pairs={{0,12},{1,13},{2,14},{3,15},{4,8},{5,9},{6,10},{7,11},{8,4},{9,5},... | collective-permute-start | bytes 1179656 | tf_op jit(solution)/shard_map/ppermute | solution.py:139
  104.8 27.9 %collective-permute-start.23 = (bf16[128,1024]{1,0:T(8,128)(2,1)}, bf16[128,1024]{1,0:T(8,128)(2,1)}, u32[]{:S(2)}, u32[]{:S(2)}) collective-permute-start(bf16[128,1024]{1,0:T(8,128)(2,1)} %get-tuple-element.99.refs_9_.refs_12_), channel_id=1, source_target_pairs={{0,4},{1,5},{2,6},{3,7},{4,0},{5,1},{6,2},{7,3},{8,12},{9,13},{10,... | collective-permute-start | bytes 786440 | tf_op jit(solution)/shard_map/ppermute | solution.py:66
  113.7 23.9 %collective-permute-start.24 = (bf16[128,1024]{1,0:T(8,128)(2,1)}, bf16[128,1024]{1,0:T(8,128)(2,1)}, u32[]{:S(2)}, u32[]{:S(2)}) collective-permute-start(bf16[128,1024]{1,0:T(8,128)(2,1)} %get-tuple-element.99.refs_9_.refs_12_), channel_id=1, source_target_pairs={{0,28},{1,29},{2,30},{3,31},{4,8},{5,9},{6,10},{7,11},{8,4},{9,5},... | collective-permute-start | bytes 786440 | tf_op jit(solution)/shard_map/ppermute | solution.py:67
  113.7 46.2 %collective-permute-start.29 = (bf16[128,1024]{1,0:T(8,128)(2,1)}, bf16[128,1024]{1,0:T(8,128)(2,1)}, u32[]{:S(2)}, u32[]{:S(2)}) collective-permute-start(bf16[128,1024]{1,0:T(8,128)(2,1)} %get-tuple-element.99.refs_9_.refs_12_), channel_id=1, source_target_pairs={{0,2},{1,3},{2,0},{3,1},{4,6},{5,7},{6,4},{7,5},{8,10},{9,11},{10,... | collective-permute-start | bytes 786440 | tf_op jit(solution)/shard_map/ppermute | solution.py:130
  121.3 49.2 %collective-permute-start.31 = (bf16[128,1024]{1,0:T(8,128)(2,1)S(1)}, bf16[128,1024]{1,0:T(8,128)(2,1)S(1)}, u32[]{:S(2)}, u32[]{:S(2)}) collective-permute-start(bf16[128,1024]{1,0:T(8,128)(2,1)S(1)} %collective-permute-done.22.refs_2_.refs_9_), channel_id=1, source_target_pairs={{0,1},{1,0},{2,3},{3,2},{4,5},{5,4},{6,7},{7,6},{8,9},{9,8},{10,11... | collective-permute-start | bytes 786440 | tf_op jit(solution)/shard_map/ppermute | solution.py:47
  129.6 46.6 %collective-permute-start.26 = (bf16[8,240,384]{2,1,0:T(8,128)(2,1)}, bf16[8,240,384]{2,1,0:T(8,128)(2,1)S(1)}, u32[]{:S(2)}, u32[]{:S(2)}) collective-permute-start(bf16[8,240,384]{2,1,0:T(8,128)(2,1)} %get-tuple-element.101.refs_1_), channel_id=1, source_target_pairs={{0,16},{16,0},{1,17},{17,1},{2,18},{18,2},{3,19},{19,3},{4,20},{20... | collective-permute-start | bytes 4423688 | tf_op jit(solution)/shard_map/ppermute | solution.py:139
  132.8 42.9 %collective-permute-start.25 = (bf16[4,192,768]{2,1,0:T(8,128)(2,1)}, bf16[4,192,768]{2,1,0:T(8,128)(2,1)S(1)}, u32[]{:S(2)}, u32[]{:S(2)}) collective-permute-start(bf16[4,192,768]{2,1,0:T(8,128)(2,1)} %get-tuple-element.100.refs_0_), channel_id=1, source_target_pairs={{0,2},{1,3},{2,0},{3,1},{4,6},{5,7},{6,4},{7,5},{8,10},{9,11},{10,... | collective-permute-start | bytes 3538952 | tf_op jit(solution)/shard_map/ppermute | solution.py:139
  149.1 22.9 %collective-permute-start.28 = (bf16[128,1024]{1,0:T(8,128)(2,1)}, bf16[128,1024]{1,0:T(8,128)(2,1)}, u32[]{:S(2)}, u32[]{:S(2)}) collective-permute-start(bf16[128,1024]{1,0:T(8,128)(2,1)} %get-tuple-element.120.refs_10_), channel_id=1, source_target_pairs={{0,2},{1,3},{2,0},{3,1},{4,6},{5,7},{6,4},{7,5},{8,10},{9,11},{10,... | collective-permute-start | bytes 786440 | tf_op jit(solution)/shard_map/ppermute | solution.py:130
  172.0 28.8 %collective-permute-start.32 = (bf16[128,1024]{1,0:T(8,128)(2,1)}, bf16[128,1024]{1,0:T(8,128)(2,1)S(1)}, u32[]{:S(2)}, u32[]{:S(2)}) collective-permute-start(bf16[128,1024]{1,0:T(8,128)(2,1)} %get-tuple-element.120.refs_10_), channel_id=1, source_target_pairs={{0,1},{1,0},{2,3},{3,2},{4,5},{5,4},{6,7},{7,6},{8,9},{9,8},{10,11... | collective-permute-start | bytes 786440 | tf_op jit(solution)/shard_map/ppermute | solution.py:47
  175.7 25.2 %collective-permute-start.35 = (bf16[128,1024]{1,0:T(8,128)(2,1)}, bf16[128,1024]{1,0:T(8,128)(2,1)S(1)}, u32[]{:S(2)}, u32[]{:S(2)}) collective-permute-start(bf16[128,1024]{1,0:T(8,128)(2,1)} %get-tuple-element.121.refs_14_), channel_id=1, source_target_pairs={{0,1},{1,0},{2,3},{3,2},{4,5},{5,4},{6,7},{7,6},{8,9},{9,8},{10,11... | collective-permute-start | bytes 786440 | tf_op jit(solution)/shard_map/ppermute | solution.py:47
  175.7 25.2 %collective-permute-start.33 = (bf16[128,1024]{1,0:T(8,128)(2,1)}, bf16[128,1024]{1,0:T(8,128)(2,1)S(1)}, u32[]{:S(2)}, u32[]{:S(2)}) collective-permute-start(bf16[128,1024]{1,0:T(8,128)(2,1)} %collective-permute-done.28.refs_11_), channel_id=1, source_target_pairs={{0,1},{1,0},{2,3},{3,2},{4,5},{5,4},{6,7},{7,6},{8,9},{9,8},{10,11... | collective-permute-start | bytes 786440 | tf_op jit(solution)/shard_map/ppermute | solution.py:47
  176.2 29.0 %collective-permute-start.36 = (bf16[128,1024]{1,0:T(8,128)(2,1)}, bf16[128,1024]{1,0:T(8,128)(2,1)S(1)}, u32[]{:S(2)}, u32[]{:S(2)}) collective-permute-start(bf16[128,1024]{1,0:T(8,128)(2,1)} %collective-permute-done.30.refs_15_), channel_id=1, source_target_pairs={{0,1},{1,0},{2,3},{3,2},{4,5},{5,4},{6,7},{7,6},{8,9},{9,8},{10,11... | collective-permute-start | bytes 786440 | tf_op jit(solution)/shard_map/ppermute | solution.py:47
  177.7 46.7 %collective-permute-start.40 = (bf16[4,240,384]{2,1,0:T(8,128)(2,1)S(1)}, bf16[4,240,384]{2,1,0:T(8,128)(2,1)S(1)}, u32[]{:S(2)}, u32[]{:S(2)}) collective-permute-start(bf16[4,240,384]{2,1,0:T(8,128)(2,1)S(1)} %get-tuple-element.118.refs_3_), channel_id=1, source_target_pairs={{0,2},{1,3},{2,0},{3,1},{4,6},{5,7},{6,4},{7,5},{8,10},{9,11},{10,... | collective-permute-start | bytes 2211848 | tf_op jit(solution)/shard_map/ppermute | solution.py:139
  200.8 22.6 %collective-permute-start.37 = (bf16[1,192,768]{2,1,0:T(8,128)(2,1)S(1)}, bf16[1,192,768]{2,1,0:T(8,128)(2,1)S(1)}, u32[]{:S(2)}, u32[]{:S(2)}) collective-permute-start(bf16[1,192,768]{2,1,0:T(8,128)(2,1)S(1)} %get-tuple-element.115.refs_0_), channel_id=1, source_target_pairs={{0,4},{1,5},{2,6},{3,7},{4,0},{5,1},{6,2},{7,3},{8,12},{9,13},{10,... | collective-permute-start | bytes 884744 | tf_op jit(solution)/shard_map/ppermute | solution.py:139
  200.8 23.5 %collective-permute-start.38 = (bf16[1,192,768]{2,1,0:T(8,128)(2,1)S(1)}, bf16[1,192,768]{2,1,0:T(8,128)(2,1)S(1)}, u32[]{:S(2)}, u32[]{:S(2)}) collective-permute-start(bf16[1,192,768]{2,1,0:T(8,128)(2,1)S(1)} %get-tuple-element.116.refs_1_), channel_id=1, source_target_pairs={{0,8},{1,9},{2,10},{3,11},{4,12},{5,13},{6,14},{7,15},{8,0},{9,1},... | collective-permute-start | bytes 884744 | tf_op jit(solution)/shard_map/ppermute | solution.py:139
  200.9 23.4 %collective-permute-start.39 = (bf16[1,192,768]{2,1,0:T(8,128)(2,1)S(1)}, bf16[1,192,768]{2,1,0:T(8,128)(2,1)S(1)}, u32[]{:S(2)}, u32[]{:S(2)}) collective-permute-start(bf16[1,192,768]{2,1,0:T(8,128)(2,1)S(1)} %get-tuple-element.117.refs_2_), channel_id=1, source_target_pairs={{0,12},{1,13},{2,14},{3,15},{4,8},{5,9},{6,10},{7,11},{8,4},{9,5},... | collective-permute-start | bytes 884744 | tf_op jit(solution)/shard_map/ppermute | solution.py:139
  223.4 23.2 %collective-permute-start.50 = (bf16[128,768]{1,0:T(8,128)(2,1)S(1)}, bf16[128,768]{1,0:T(8,128)(2,1)S(1)}, u32[]{:S(2)}, u32[]{:S(2)}) collective-permute-start(bf16[128,768]{1,0:T(8,128)(2,1)S(1)} %copy-done.21), channel_id=1, source_target_pairs={{0,1},{1,0},{2,3},{3,2},{4,5},{5,4},{6,7},{7,6},{8,9},{9,8},{10,11... | collective-permute-start | bytes 589832 | tf_op jit(solution)/shard_map/ppermute | solution.py:47
  224.4 22.3 %collective-permute-start.51 = (bf16[2,128,768]{2,1,0:T(8,128)(2,1)S(1)}, bf16[2,128,768]{2,1,0:T(8,128)(2,1)S(1)}, u32[]{:S(2)}, u32[]{:S(2)}) collective-permute-start(bf16[2,128,768]{2,1,0:T(8,128)(2,1)S(1)} %copy-done.24), channel_id=1, source_target_pairs={{0,1},{1,0},{2,3},{3,2},{4,5},{5,4},{6,7},{7,6},{8,9},{9,8},{10,11... | collective-permute-start | bytes 1179656 | tf_op jit(solution)/shard_map/ppermute | solution.py:47
  265.0 23.3 %collective-permute-start.57 = (bf16[1,240,384]{2,1,0:T(8,128)(2,1)S(1)}, bf16[1,240,384]{2,1,0:T(8,128)(2,1)S(1)}, u32[]{:S(2)}, u32[]{:S(2)}) collective-permute-start(bf16[1,240,384]{2,1,0:T(8,128)(2,1)S(1)} %get-tuple-element.142), channel_id=1, source_target_pairs={{0,8},{1,9},{2,10},{3,11},{4,12},{5,13},{6,14},{7,15},{8,0},{9,1},... | collective-permute-start | bytes 552968 | tf_op jit(solution)/shard_map/ppermute | solution.py:139
  265.1 23.2 %collective-permute-start.58 = (f32[184,128]{1,0:T(8,128)S(1)}, f32[184,128]{1,0:T(8,128)S(1)}, u32[]{:S(2)}, u32[]{:S(2)}) collective-permute-start(f32[184,128]{1,0:T(8,128)S(1)} %get-tuple-element.141.refs_2_), channel_id=1, source_target_pairs={{0,8},{1,9},{2,10},{3,11},{4,12},{5,13},{6,14},{7,15},{8,0},{9,1},... | collective-permute-start | bytes 282632 | tf_op jit(solution)/shard_map/ppermute | solution.py:139
  (101 other events, 1194.2 us)
